TPU v7x, 32 devices: a whole 2x2x4 slice. The times are simulated.
32 devices in a mesh: dp: 8 (over z, y), tensor: 4 (over x, core).
Axes of the slice: x: 2, y: 2, z: 4, core: 2. Of those that a mesh axis runs over, the one named last changes fastest.
Arguments:
- tokens: bfloat16 [8, 1536, 1024], P('dp'), may hold values from -6 to 6
- cotangent: bfloat16 [8, 1536, 1024], P('dp'), may hold values from -12 to 12
- parents: int32 [8, 13], replicated, may hold values from 0 to 4, as said below
- token_segment: int32 [8, 1536], P('dp'), may hold values from 0 to 12, never falling along the last dimension, each value on 1 to 384 neighbouring positions
- tree_id: int32 [8], P('dp'), may hold values from 0 to 7
- projection_weight: float32 [1024, 8, 4, 128], P('dp', 'tensor'), may hold values from -0.1875 to 0.1875
- projection_first_moment: float32 [1024, 8, 4, 128], P('dp', 'tensor'), may hold values from -1280 to 1280
- projection_second_moment: float32 [1024, 8, 4, 128], P('dp', 'tensor'), may hold values from 49152 to 196608
- merge_master: float32 [2048, 1024], P('tensor', 'dp'), may hold values from -0.75 to 0.75
- merge_mean: float32 [2048, 1024], P('tensor', 'dp'), may hold values from -160 to 160
- merge_square: float32 [2048, 1024], P('tensor', 'dp'), may hold values from 384 to 3072
- expand_master: float32 [1024, 2, 3072], P('dp', None, 'tensor'), may hold values from -0.1875 to 0.1875
- expand_mean: float32 [1024, 2, 3072], P('dp', None, 'tensor'), may hold values from -384 to 384
- expand_square: float32 [1024, 2, 3072], P('dp', None, 'tensor'), may hold values from 2048 to 12288
- shrink_master: float32 [3072, 1024], P('tensor', 'dp'), may hold values from -0.109375 to 0.109375
- shrink_mean: float32 [3072, 1024], P('tensor', 'dp'), may hold values from -640 to 640
- shrink_square: float32 [3072, 1024], P('tensor', 'dp'), may hold values from 6144 to 49152
- gain_master: float32 [2304], replicated, may hold values from 0.5 to 1.5
- gain_mean: float32 [2304], replicated, may hold values from -640 to 640
- gain_square: float32 [2304], replicated, may hold values from 3072 to 49152
Outputs:
- output: bfloat16 [8, 1536, 1024], P('dp', 'tensor')
- input_grad: bfloat16 [8, 1536, 1024], P('dp', 'tensor')
- project_next: float32 [1024, 8, 4, 128], P('dp', 'tensor')
- project_mean_next: float32 [1024, 8, 4, 128], P('dp', 'tensor')
- project_square_next: float32 [1024, 8, 4, 128], P('dp', 'tensor')
- project_copy: bfloat16 [1024, 8, 4, 128], P('dp', 'tensor')
- merge_next: float32 [2048, 1024], P('tensor', 'dp')
- merge_mean_next: float32 [2048, 1024], P('tensor', 'dp')
- merge_square_next: float32 [2048, 1024], P('tensor', 'dp')
- merge_copy: bfloat16 [2048, 1024], P('tensor', 'dp')
- expand_next: float32 [1024, 2, 3072], P('dp', None, 'tensor')
- expand_mean_next: float32 [1024, 2, 3072], P('dp', None, 'tensor')
- expand_square_next: float32 [1024, 2, 3072], P('dp', None, 'tensor')
- expand_copy: bfloat16 [1024, 2, 3072], P('dp', None, 'tensor')
- shrink_next: float32 [3072, 1024], P('tensor', 'dp')
- shrink_mean_next: float32 [3072, 1024], P('tensor', 'dp')
- shrink_square_next: float32 [3072, 1024], P('tensor', 'dp')
- shrink_copy: bfloat16 [3072, 1024], P('tensor', 'dp')
- gain_mean_next: float32 [2304], replicated
- gain_square_next: float32 [2304], replicated
- gain_next: float32 [2304], replicated
Inputs may be any that keep to these rules, and one draw needn't show every extreme that they name: `parents`: in each row segment 0 is the trunk and its own parent, segments 1 to 4 have parent 0, and every later segment has a parent among 1 to 4. `token_segment`: within a tree the segment numbers never fall and all 13 segments are present.
All inputs are finite; a program needn't handle non-finite values.
Results may differ from a plain program's by a relative error of at most 0.015.
Values may be sent and summed in bfloat16 or wider, within the bound.
A program may use at most 192 MiB of HBM per device.

v0:
```python
import math
from functools import partial

import jax
import jax.numpy as jnp
import numpy as np
from jax import lax
from jax.experimental import pallas as pl
from jax.experimental.pallas import tpu as pltpu
from jax.sharding import PartitionSpec as P

STEP = 5
EPS_NORM = 1e-06
THETA = 1000000.0
BETA_ONE = 0.5
BETA_TWO = 0.5
EPS_ADAM = 1e-08
DECAY = 0.1
RATE_PROJECT = 0.05
RATE_MERGE = 0.3
RATE_EXPAND = 0.05
RATE_SHRINK = 0.03
RATE_GAIN = 0.3

BF = jnp.bfloat16
FP = jnp.float32
ROWS = 256
LANES = 128
SUB = 128
MESH = pl.DeviceIdType.MESH
BLOCKED = -1e30
VMEM_LIMIT = 56 * 2**20


def params(**more):
    return pltpu.CompilerParams(vmem_limit_bytes=VMEM_LIMIT, **more)


def dot(a, b, ca=1, cb=0):
    return lax.dot_general(a, b, (((ca,), (cb,)), ((), ())), preferred_element_type=FP)


def inverse_rms(values):
    return lax.rsqrt(jnp.mean(values * values, axis=-1, keepdims=True) + EPS_NORM)


def rms_pull(values, scales, grad):
    r = inverse_rms(values)
    scaled = grad * scales
    mean = jnp.mean(values * scaled, axis=-1, keepdims=True)
    return r * scaled - values * (r * r * r * mean), grad * values * r


def fold_rows(values):
    n, w = values.shape
    return jnp.sum(values.reshape(n // 8, 8, w), axis=0)


class Place:
    def __init__(self, line):
        self.line = line
        self.dp, self.t = lax.axis_index("dp"), lax.axis_index("tensor")
        self.z, self.y = self.dp // 2, self.dp % 2
        self.x, self.c = self.t // 2, self.t % 2
        self.has_up, self.has_down = self.z < line - 1, self.z > 0
        self.up, self.down = (self.dp + 2, self.t), (self.dp - 2, self.t)
        self.across = (self.dp + 1 - 2 * self.y, self.t)
        self.sibling = (self.dp, self.t + 1 - 2 * self.c)
        self.chip = (self.dp, (1 - self.x) * 2 + self.c)

    def greet(self, tensor, line, meanwhile=None):
        barrier = pltpu.get_barrier_semaphore()

        def signal(device):
            pl.semaphore_signal(barrier, inc=1, device_id=device, device_id_type=MESH)

        if tensor:
            signal(self.sibling)
            signal(self.chip)
        if line:
            signal(self.across)
            pl.when(self.has_up)(lambda: signal(self.up))
            pl.when(self.has_down)(lambda: signal(self.down))
        peers = (2 if tensor else 0) + (1 if line else 0)
        if line:
            peers = peers + jnp.where(self.has_up, 1, 0) + jnp.where(self.has_down, 1, 0)
        if meanwhile is not None:
            meanwhile()
        pl.semaphore_wait(barrier, peers)


def send(src, dst, sent, arrived, device):
    return pltpu.make_async_remote_copy(
        src_ref=src, dst_ref=dst, send_sem=sent, recv_sem=arrived, device_id=device, device_id_type=MESH)


def row_cut(size):
    return lambda j: (pl.ds(pl.multiple_of(j * size, size), size), slice(None))


def column_cut(size):
    return lambda j: (slice(None), pl.ds(pl.multiple_of(j * size, size), size))


class Gather:
    def __init__(self, place, own, full, cut, sems, local):
        self.place, self.own, self.full, self.cut, self.sems, self.local = place, own, full, cut, sems, local

    def copy(self, kind, src, j):
        p = self.place
        device = (p.up, p.down, p.across)[kind]
        return send(src, self.full.at[self.cut(j)], self.sems.at[kind, j], self.sems.at[3, j], device)

    def kept(self):
        return pltpu.make_async_copy(self.own, self.full.at[self.cut(self.place.dp)], self.local)

    def source(self):
        return self.full.at[self.cut(self.place.dp)] if self.own is None else self.own

    def start(self):
        p = self.place
        self.copy(2, self.source(), p.dp).start()
        pl.when(p.has_up)(lambda: self.copy(0, self.source(), p.dp).start())
        pl.when(p.has_down)(lambda: self.copy(1, self.source(), p.dp).start())
        if self.own is not None:
            self.kept().start()

    def arrivals(self, k):
        p = self.place
        return ((0, p.z >= k, (p.z - k) * 2 + p.y, p.has_up), (1, p.z + k < p.line, (p.z + k) * 2 + p.y, p.has_down))

    def hop(self, k):
        for kind, here, j, further in self.arrivals(k):
            @pl.when(here)
            def _(kind=kind, j=j, further=further):
                piece = self.full.at[self.cut(j)]
                self.copy(kind, piece, j).wait_recv()
                pl.when(further)(lambda: self.copy(kind, piece, j).start())
                self.copy(2, piece, j).start()

    def finish(self):
        p = self.place
        if self.own is not None:
            self.kept().wait()
        for zz in range(p.line):
            j = zz * 2 + 1 - p.y
            self.copy(2, self.full.at[self.cut(j)], j).wait_recv()

    def drain(self):
        p = self.place
        self.copy(2, self.source(), p.dp).wait_send()
        pl.when(p.has_up)(lambda: self.copy(0, self.source(), p.dp).wait_send())
        pl.when(p.has_down)(lambda: self.copy(1, self.source(), p.dp).wait_send())
        for k in range(1, p.line):
            for kind, here, j, further in self.arrivals(k):
                @pl.when(here)
                def _(kind=kind, j=j, further=further):
                    piece = self.full.at[self.cut(j)]
                    pl.when(further)(lambda: self.copy(kind, piece, j).wait_send())
                    self.copy(2, piece, j).wait_send()


class Reduce:
    def __init__(self, place, grad, cut, kept, across, lined, sems):
        self.place, self.grad, self.cut, self.kept, self.sems = place, grad, cut, kept, sems
        self.across, self.lined = across, lined

    def cross(self, zz):
        p = self.place
        return send(self.grad.at[self.cut(zz * 2 + 1 - p.y)], self.across.at[zz],
                    self.sems.at[0, zz], self.sems.at[1, zz], p.across)

    def climb(self, t):
        return send(self.across.at[t], self.lined.at[t + 1], self.sems.at[2, t], self.sems.at[3, t], self.place.up)

    def sink(self, t):
        return send(self.across.at[t], self.lined.at[t], self.sems.at[4, t], self.sems.at[5, t], self.place.down)

    def load(self, zz):
        return pltpu.make_async_copy(self.grad.at[self.cut(zz * 2 + self.place.y)], self.kept.at[zz], self.sems.at[6, zz])

    def mine(self, zz):
        if self.kept is None:
            return self.grad[self.cut(zz * 2 + self.place.y)].astype(FP)
        return self.kept[zz].astype(FP)

    def loaded(self, zz):
        if self.kept is not None:
            self.load(zz).wait()

    def turn(self, q):
        z = self.place.z
        low = z < 2
        if q == 0:
            return jnp.where(low, 3, 0)
        if q == 1:
            return jnp.where(low, 2, 1)
        if q == 2:
            return jnp.where(low, 1 - z, 5 - z)
        return z

    def start(self):
        self.cross(self.turn(0)).start()
        if self.kept is not None:
            for zz in range(self.place.line):
                self.load(zz).start()

    def advance(self, q):
        self.cross(self.turn(q - 1)).wait_send()
        self.cross(self.turn(q)).start()

    def hop(self, h):
        p = self.place

        def pass_on(t, coming, more, slot):
            self.loaded(t)
            self.cross(t).wait_recv()

            @pl.when(jnp.logical_not(more))
            def _():
                self.across[t] = (self.mine(t) + self.across[t].astype(FP)).astype(BF)

            @pl.when(more)
            def _():
                coming(t).wait_recv()
                self.across[t] = (self.mine(t) + self.across[t].astype(FP) + self.lined[slot].astype(FP)).astype(BF)

            coming(t).start()

        pl.when(p.z < h)(lambda: pass_on(p.z + p.line - h, self.climb, p.has_down, p.z + p.line - h + 1))
        pl.when(p.z >= p.line - h)(lambda: pass_on(p.z - p.line + h, self.sink, p.has_up, p.z - p.line + h))

    def finish(self, write):
        p = self.place
        self.loaded(p.z)
        self.cross(p.z).wait_recv()
        pl.when(p.has_down)(lambda: self.climb(p.z).wait_recv())
        pl.when(p.has_up)(lambda: self.sink(p.z).wait_recv())
        from_below = jnp.where(p.has_down, self.lined[p.z + 1].astype(FP), 0.0)
        from_above = jnp.where(p.has_up, self.lined[p.z].astype(FP), 0.0)
        write(self.mine(p.z) + self.across[p.z].astype(FP) + from_below + from_above)

    def step(self, k):
        self.advance(k)
        self.hop(k)

    def drain(self):
        p = self.place
        self.cross(p.z).wait_send()
        for zz in range(p.line):
            pl.when(zz > p.z)(lambda zz=zz: self.climb(zz).wait_send())
            pl.when(zz < p.z)(lambda zz=zz: self.sink(zz).wait_send())


def write_to(ref):
    def write(values):
        if len(ref.shape) == 2:
            ref[...] = values
            return
        width = ref.shape[2]
        for j in range(ref.shape[1]):
            ref[:, j, :] = values[:, j * width:(j + 1) * width]

    return write


def reduce_scratch(line, shape, kept=False):
    return [pltpu.VMEM((line, *shape), BF)] * kept + [pltpu.VMEM((line, *shape), BF), pltpu.VMEM((line + 1, *shape), BF),
                                                      pltpu.SemaphoreType.DMA((7, line))]


class Pairs:
    def __init__(self, place, per, held, near, sems, slot_of):
        self.place, self.per, self.held, self.near, self.sems, self.slot_of = place, per, held, near, sems, slot_of

    def near_slot(self, s):
        return (s // (2 * self.per)) * self.per + s % self.per

    def to_sibling(self, s):
        return send(self.held.at[self.slot_of(s)], self.near.at[self.near_slot(s)], self.sems.at[0, s],
                    self.sems.at[1, s], self.place.sibling)

    def sends(self, s):
        return self.place.c != (s // self.per) % 2

    def sent(self, s):
        pl.when(self.sends(s))(lambda: self.to_sibling(s).wait_send())

    def put(self, s, rows, before=None):
        if before is not None:
            pl.when(before[0])(lambda: self.sent(before[1]))
        self.held[self.slot_of(s)] = rows
        pl.when(self.sends(s))(lambda: self.to_sibling(s).start())

    def put_next(self, s, rows):
        self.put(s, rows, (s % self.per >= 1, s - 1))

    def add(self, s, use):
        t = s // self.per

        @pl.when(self.place.c == t % 2)
        def _():
            self.to_sibling(s).wait_recv()
            use(self.place.x == t // 2, s % self.per,
                self.held[self.slot_of(s)].astype(FP) + self.near[self.near_slot(s)].astype(FP))


class Exchange(Pairs):
    def __init__(self, place, per, held, near, far, total, sems):
        super().__init__(place, per, held, near, sems, lambda s: s // per)
        self.far, self.total = far, total

    def rows(self, k):
        return pl.ds(pl.multiple_of(k * SUB, SUB), SUB)

    def to_chip(self, s):
        return send(self.near.at[self.near_slot(s)], self.far.at[s % self.per], self.sems.at[2, s], self.sems.at[3, s],
                    self.place.chip)

    def add_chip(self, s):
        def use(mine, k, summed):
            @pl.when(jnp.logical_not(mine))
            def _():
                self.near[self.near_slot(s)] = summed.astype(BF)
                self.to_chip(s).start()

            @pl.when(mine)
            def _():
                self.total[self.rows(k), :] = summed

        self.add(s, use)

    def take(self, s, use):
        @pl.when(s // self.per == self.place.t)
        def _():
            k = s % self.per
            self.to_chip(s).wait_recv()
            use(s, self.rows(k), self.total[self.rows(k), :] + self.far[k].astype(FP))

    def drain(self):
        p = self.place

        def one(s, carry):
            t = s // self.per
            pl.when(s % self.per == self.per - 1)(lambda: self.sent(s))
            pl.when(jnp.logical_and(p.c == t % 2, p.x != t // 2))(lambda: self.to_chip(s).wait_send())
            return carry

        lax.fori_loop(0, 4 * self.per, one, 0)


def pair_of(step, per):
    t = step % 2
    return t * per + step // 2, (3 - t) * per + step // 2


def pairs_scratch(per, d, exchange):
    rows = [pltpu.VMEM((4, SUB, d), BF), pltpu.VMEM((2 * per, SUB, d), BF)]
    return rows + [pltpu.VMEM((per, SUB, d), BF)] * exchange + [pltpu.SemaphoreType.DMA((4 if exchange else 2, 4 * per))]


class Spread:
    def __init__(self, place, per, stage, full, sems):
        self.place, self.per, self.stage, self.full, self.sems = place, per, stage, full, sems

    def rows(self, s):
        return self.full.at[pl.ds(pl.multiple_of(s * SUB, SUB), SUB), :]

    def source(self, s):
        return self.rows(s) if self.stage is None else self.stage.at[s % self.per]

    def copy(self, kind, src, s):
        device = (self.place.chip, self.place.sibling)[kind]
        return send(src, self.rows(s), self.sems.at[kind, s], self.sems.at[2, s], device)

    def kept(self, s):
        return pltpu.make_async_copy(self.source(s), self.rows(s), self.sems.at[3, s])

    def send(self, s):
        for kind in (0, 1):
            self.copy(kind, self.source(s), s).start()
        if self.stage is not None:
            self.kept(s).start()

    def owns(self, s):
        return s // self.per == self.place.t

    def passes(self, s):
        t = s // self.per
        return jnp.logical_and(self.place.c == t % 2, self.place.x != t // 2)

    def pass_on(self, s):
        @pl.when(self.passes(s))
        def _():
            self.copy(1, self.rows(s), s).wait_recv()
            self.copy(1, self.rows(s), s).start()

    def ready(self, s):
        if self.stage is not None:
            pl.when(self.owns(s))(lambda: self.kept(s).wait())
        pl.when((s // self.per) % 2 != self.place.c)(lambda: self.copy(1, self.rows(s), s).wait_recv())

    def drain(self):
        def one(s, carry):
            @pl.when(self.owns(s))
            def _():
                self.copy(0, self.source(s), s).wait_send()
                self.copy(1, self.source(s), s).wait_send()

            pl.when(self.passes(s))(lambda: self.copy(1, self.rows(s), s).wait_send())
            return carry

        lax.fori_loop(0, 4 * self.per, one, 0)


def whole(shape):
    return pl.BlockSpec(tuple(shape), lambda i: (0,) * len(shape), pipeline_mode=pl.Buffered(1))


ANYWHERE = pl.BlockSpec(memory_space=pl.ANY)
GATHER_SEMS = lambda shards: [pltpu.SemaphoreType.DMA((4, shards)), pltpu.SemaphoreType.DMA]


def make_tables(seg_ref, parents_ref, tree_ref, freq_ref, tags_ref, bars_ref, cos_ref, sin_ref):
    count = parents_ref.shape[1]
    n = LANES
    blocks = sin_ref.shape[0] // ROWS
    lane = lax.broadcasted_iota(jnp.int32, (1, n), 1).astype(FP)
    place_of = lambda b: pl.ds(pl.multiple_of(b * ROWS, ROWS), ROWS)

    def columns(b, carry):
        sin_ref[place_of(b), :] = jnp.broadcast_to(seg_ref[:, place_of(b)].astype(FP), (n, ROWS)).T
        return carry

    def tally(b, carry):
        column = sin_ref[place_of(b), :]
        return (carry[0] + fold_rows(jnp.where(column == lane, 1.0, 0.0)),
                carry[1] + fold_rows(jnp.where(column < lane, 1.0, 0.0)))

    lax.fori_loop(0, blocks, columns, 0)
    sizes, starts = lax.fori_loop(0, blocks, tally, (jnp.zeros((8, n), FP), jnp.zeros((8, n), FP)))
    sizes, starts = (jnp.sum(a, axis=0, keepdims=True) for a in (sizes, starts))
    table = parents_ref[...]
    chosen = jnp.where(lax.broadcasted_iota(jnp.int32, table.shape, 0) == tree_ref[0], table, 0)
    chosen = jnp.sum(chosen.astype(FP), axis=0, keepdims=True)
    parents = jnp.zeros((1, n), FP)
    for b in range(count):
        parents = jnp.where(lane == b, chosen[:, b:b + 1], parents)
    shifts = jnp.where(lane != 0, sizes[:, :1], 0.0) - starts

    def rows(b, carry):
        at = place_of(b)
        column = sin_ref[at, :]
        hot = column == lane
        parent = jnp.sum(jnp.where(hot, parents, 0.0), axis=1, keepdims=True)
        above = jnp.where(jnp.logical_and(lane == parent, lane != 0), sizes, 0.0)
        first = (b * ROWS).astype(FP)
        position = (lax.broadcasted_iota(jnp.int32, (ROWS, 1), 0).astype(FP) + first
                    + jnp.sum(jnp.where(hot, shifts, 0.0) + above, axis=1, keepdims=True))
        tags_ref[at, :] = jnp.where(hot, 1.0, 0.0).astype(BF)
        open_to = jnp.logical_or(jnp.logical_or(hot, lane == parent), jnp.logical_or(lane == 0, lane >= count))
        bars_ref[at, :] = jnp.where(open_to, 0.0, BLOCKED).astype(BF)
        angles = position * freq_ref[...]
        cos_ref[at, :] = jnp.cos(angles)
        turned = jnp.sin(angles)
        sin_ref[at, :] = jnp.where(lane < n // 2, -turned, turned)
        return carry

    lax.fori_loop(0, blocks, rows, 0)


def front_kernel(kv, group, line, *refs):
    refs = list(refs)
    take = lambda count: [refs.pop(0) for _ in range(count)]
    x_ref, gains_ref, seg_ref, parents_ref, tree_ref, freq_ref = take(6)
    masters = take(4) if line else take(1)
    xn_ref, q_ref, k_ref, v_ref, kt_ref, vt_ref, raw_ref, tags_ref, bars_ref, cos_ref, sin_ref = take(11)
    if line:
        wp_out, wm_out, we_low, ws_low = take(4)
        wp_ref, wm_low, p_sems, p_local, m_sems, m_local, out_sem = take(7)
    else:
        wp_ref = masters[0]
    xn_full, xn_sem = take(2)
    i = pl.program_id(0)
    final = pl.num_programs(0) - 1
    d = x_ref.shape[1]
    n = LANES
    per = group + 2
    if line:
        place = Place(line)
        size = masters[0].shape[0]
        project = Gather(place, None, wp_ref, row_cut(size), p_sems, p_local)
        merge = Gather(place, wm_low, wm_out, column_cut(wm_low.shape[1]), m_sems, m_local)
        written = pltpu.make_async_copy(wp_ref, wp_out, out_sem)
    normed = pltpu.make_async_copy(xn_full, xn_ref, xn_sem)

    def round_projection():
        at = pl.ds(pl.multiple_of(place.dp * size, size), size)
        for j in range(kv * per):
            wp_ref[at, j * n:(j + 1) * n] = masters[0][:, j, :].astype(BF)

    def norm(b, carry):
        at = pl.ds(pl.multiple_of(b * ROWS, ROWS), ROWS)
        x = x_ref[at, :].astype(FP)
        xn_full[at, :] = (x * inverse_rms(x) * gains_ref[:, :d]).astype(BF)
        return carry

    @pl.when(i == 0)
    def _():
        if line:
            place.greet(False, True, round_projection)
            project.start()
        lax.fori_loop(0, x_ref.shape[0] // ROWS, norm, 0)
        normed.start()
        if line:
            project.hop(1)
        make_tables(seg_ref, parents_ref, tree_ref, freq_ref, tags_ref, bars_ref, cos_ref, sin_ref)
        if line:
            project.hop(2)
            wm_low[...] = masters[1][...].astype(BF)
            units = masters[2].shape[2]
            for half in range(2):
                we_low[:, half * units:(half + 1) * units] = masters[2][:, half, :].astype(BF)
            ws_low[...] = masters[3][...].astype(BF)
            project.hop(3)
            merge.start()
            project.finish()
            written.start()

    if line:
        for k in range(1, line):
            pl.when(i == k + 1)(lambda k=k: merge.hop(k))
    at = pl.ds(pl.multiple_of(i * ROWS, ROWS), ROWS)
    qkv = dot(xn_full[at, :], wp_ref[...])
    cosines, sines = cos_ref[at, :], sin_ref[at, :]
    gq, gk = gains_ref[:, 2 * d:2 * d + n], gains_ref[:, 2 * d + n:]
    keys, values = [], []
    for h in range(kv):
        for c in range(group + 1):
            raw = qkv[:, (h * per + c) * n:(h * per + c + 1) * n]
            to = (h * (group + 1) + c) * n
            raw_ref[:, to:to + n] = raw
            y = raw * inverse_rms(raw) * (gq if c < group else gk)
            turned = y * cosines + pltpu.roll(y, n // 2, 1) * sines
            if c < group:
                to = (h * group + c) * n
                q_ref[:, to:to + n] = turned.astype(BF)
            else:
                keys.append(turned)
        values.append(qkv[:, (h * per + group + 1) * n:(h * per + group + 2) * n])
    for h in range(kv):
        k_ref[:, h * n:(h + 1) * n] = keys[h].astype(BF)
        v_ref[:, h * n:(h + 1) * n] = values[h].astype(BF)
        kt_ref[h * n:(h + 1) * n, :] = keys[h].T.astype(BF)
        vt_ref[h * n:(h + 1) * n, :] = values[h].T.astype(BF)

    @pl.when(i == final)
    def _():
        normed.wait()
        if line:
            merge.finish()
            merge.drain()
            project.drain()
            written.wait()


def front(x, gains, segments, parents, tree, masters, kv, group, line):
    length, d = x.shape
    n = LANES
    rows = lambda w: pl.BlockSpec((ROWS, w), lambda i: (i, 0))
    cols = pl.BlockSpec((kv * n, ROWS), lambda i: (0, i))
    out = lambda w, t: jax.ShapeDtypeStruct((length, w), t)
    raw_w = kv * (group + 1) * n
    freq = np.float32(THETA ** (-(np.arange(n) % (n // 2)) * 2.0 / n))[None]
    more_specs, more_shapes, scratch = [], [], []
    if line:
        shards = 2 * line
        project, merge, expand, shrink = (m.shape for m in masters)
        wp_shape = (project[0] * shards, project[1] * n)
        more_shapes = [jax.ShapeDtypeStruct(wp_shape, BF), jax.ShapeDtypeStruct((merge[0], merge[1] * shards), BF),
                       jax.ShapeDtypeStruct((expand[0], 2 * expand[2]), BF), jax.ShapeDtypeStruct(shrink, BF)]
        more_specs = [ANYWHERE, ANYWHERE, whole(more_shapes[2].shape), whole(more_shapes[3].shape)]
        scratch = [pltpu.VMEM(wp_shape, BF), pltpu.VMEM(merge, BF), *GATHER_SEMS(shards), *GATHER_SEMS(shards),
                   pltpu.SemaphoreType.DMA]
    table = whole((length, n))
    return pl.pallas_call(
        partial(front_kernel, kv, group, line),
        grid=(length // ROWS,),
        in_specs=[whole(x.shape), whole(gains.shape), whole(segments.shape), whole(parents.shape),
                  pl.BlockSpec(memory_space=pltpu.SMEM), whole(freq.shape), *[whole(m.shape) for m in masters]],
        out_specs=[ANYWHERE, rows(kv * group * n), rows(kv * n), rows(kv * n), cols, cols, rows(raw_w),
                   table, table, table, table, *more_specs],
        out_shape=[out(d, BF), out(kv * group * n, BF), out(kv * n, BF), out(kv * n, BF),
                   jax.ShapeDtypeStruct((kv * n, length), BF), jax.ShapeDtypeStruct((kv * n, length), BF),
                   out(raw_w, FP), out(n, BF), out(n, BF), out(n, FP), out(n, FP), *more_shapes],
        scratch_shapes=[*scratch, pltpu.VMEM((length, d), BF), pltpu.SemaphoreType.DMA],
        compiler_params=params(**({"collective_id": 0, "has_side_effects": True} if line else {})),
        name="front",
    )(x, gains, segments, parents, tree, freq, *masters)


def stacked(ref_block, h, group):
    n = LANES
    return jnp.concatenate(
        [ref_block[:, (h * group + g) * n:(h * group + g + 1) * n] for g in range(group)], axis=0)


def causal_tile(group, rows=ROWS, after=0):
    key_at = lax.broadcasted_iota(jnp.int32, (ROWS, rows * group), 0)
    query_at = lax.broadcasted_iota(jnp.int32, (ROWS, rows * group), 1) % rows
    return key_at <= query_at + after


def in_turn(i, first, steps, per, acts):
    for behind, act in acts:
        @pl.when(jnp.logical_and(i - first - behind >= 0, i - first - behind < steps))
        def _(behind=behind, act=act):
            for s in pair_of(i - first - behind, per):
                act(s)


def middle_kernel(kv, group, unit, line, per, steps, *refs):
    refs = list(refs)
    take = lambda count: [refs.pop(0) for _ in range(count)]
    q_ref, k_ref, vt_ref, tags_ref, bars_ref, wm_ref, gains_ref, x_all, dy_all = take(9)
    weights = take(2)
    ctx_ref, lse_ref, base_ref, other_ref, gex_ref, dh_ref, dhb_ref, dg_ref, gsh_out = take(9)
    acc_ref, sum_ref, x_ref, dy_ref, we_ref, ws_ref, copy_sems = take(7)
    h_ref, xn_ref, a_ref, dgu_ref = take(4)
    h_held, h_near, h_far, h_sems, xn_sems = take(5)
    d_held, d_near, d_far, d_sems, stage, dh_sems = take(6)
    b_held, b_near, b_sems = take(3)
    place = Place(line)
    i = pl.program_id(0)
    n = LANES
    share, d = x_ref.shape
    units = ws_ref.shape[0]
    tile = 256
    attended = Exchange(place, per, h_held, h_near, h_far, h_ref, h_sems)
    norms = Spread(place, per, None, xn_ref, xn_sems)
    pulled_back = Exchange(place, per, d_held, d_near, d_far, dh_ref, d_sems)
    grads = Spread(place, per, stage, dhb_ref, dh_sems)
    branch = Pairs(place, per, b_held, b_near, b_sems, lambda s: s // per)
    own_share = x_all.at[pl.ds(pl.multiple_of(place.t * share, share), share), :]
    copies = [pltpu.make_async_copy(own_share, x_ref, copy_sems.at[0]),
              pltpu.make_async_copy(dy_all, dy_ref, copy_sems.at[1])]
    if line:
        gsh_ref = take(1)[0]
        shrink = Reduce(place, gsh_ref, column_cut(gsh_ref.shape[1] // (2 * line)), None, *take(3))
        cuts = (row_cut(weights[0].shape[0]), column_cut(weights[1].shape[1]))
        first, second = [Gather(place, weights[w], (we_ref, ws_ref)[w], cuts[w], *take(2)) for w in range(2)]
    else:
        gsh_ref = gsh_out
        copies += [pltpu.make_async_copy(weights[0], we_ref, copy_sems.at[2]),
                   pltpu.make_async_copy(weights[1], ws_ref, copy_sems.at[3])]
    rows_of = lambda s: pl.ds(pl.multiple_of(s * SUB, SUB), SUB)

    def at_step(step, *acts):
        @pl.when(i == step)
        def _():
            for act in acts:
                act()

    @pl.when(i == 0)
    def _():
        place.greet(True, bool(line))
        if line:
            first.start()
        for copy in copies:
            copy.start()
        dg_ref[...] = jnp.zeros_like(dg_ref)


    def block(s):
        here = rows_of(s)
        bars = jnp.concatenate([bars_ref[here, :]] * group, axis=0)
        q = q_ref[here, :]
        wide = [jnp.concatenate([stacked(q, h, group), bars], axis=1) for h in range(kv)]
        acc_ref[...] = jnp.zeros_like(acc_ref)
        sum_ref[...] = jnp.zeros_like(sum_ref)

        def chunk(j, diagonal):
            at = pl.ds(pl.multiple_of(j * ROWS, ROWS), ROWS)
            tags = tags_ref[at, :]
            for h in range(kv):
                keys = jnp.concatenate([k_ref[at, h * n:(h + 1) * n], tags], axis=1)
                scores = dot(keys, wide[h], 1, 1)
                e = jnp.exp2(scores * unit)
                if diagonal:
                    e = jnp.where(causal_tile(group, SUB, (s % 2) * SUB), e, 0.0)
                sum_ref[h] += fold_rows(e)
                acc_ref[h] += dot(vt_ref[h * n:(h + 1) * n, at], e.astype(BF))

        lax.fori_loop(0, s // 2, lambda j, c: (chunk(j, False), c)[1], 0)
        chunk(s // 2, True)
        parts = []
        for h in range(kv):
            sums = jnp.sum(sum_ref[h], axis=0, keepdims=True)
            lse_ref[s, h:h + 1, :] = jnp.log2(sums)
            ctx = (acc_ref[h] / sums).T
            parts += [ctx[g * SUB:(g + 1) * SUB] for g in range(group)]
        ctx_ref[here, :] = jnp.concatenate(parts, axis=1).astype(BF)

    def put_pair(pairs, blocks, part):
        for u, s in enumerate(blocks):
            pairs.put_next(s, part[u * SUB:(u + 1) * SUB])

    @pl.when(i < steps)
    def _():
        blocks = pair_of(i, per)
        for s in blocks:
            block(s)
        ctx = jnp.concatenate([ctx_ref[rows_of(s), :] for s in blocks], axis=0)
        put_pair(attended, blocks, dot(ctx, wm_ref[...]).astype(BF))

    def hidden_rows(s, at, summed):
        hidden = x_ref[at, :].astype(FP) + summed
        h_ref[at, :] = hidden
        xn_ref[rows_of(s), :] = (hidden * inverse_rms(hidden) * gains_ref[:, d:2 * d]).astype(BF)
        norms.send(s)

    at_step(1, copies[0].wait)
    in_turn(i, 0, steps, per, ((1, attended.add_chip), (3, lambda s: attended.take(s, hidden_rows)), (5, norms.pass_on)))
    swiglu, feed = steps + 3, 2 * steps + 3
    if line:
        at_step(1, lambda: first.hop(1))
        at_step(3, lambda: first.hop(2))
        at_step(5, lambda: first.hop(3), second.start)
        at_step(7, lambda: second.hop(1))
        at_step(8, lambda: second.hop(2))
        at_step(9, lambda: second.hop(3), first.finish)
        at_step(feed, second.finish)
    else:
        at_step(swiglu, copies[2].wait, copies[3].wait)


    def opened(blocks):
        xn = jnp.concatenate([xn_ref[rows_of(s), :] for s in blocks], axis=0)
        gu = dot(xn, we_ref[...])
        gate, up = gu[:, :units], gu[:, units:]
        sig = 1.0 / (1.0 + jnp.exp(-gate))
        return gate, up, sig

    def keep(ref, blocks, values):
        for u, s in enumerate(blocks):
            ref[rows_of(s), :] = values[u * SUB:(u + 1) * SUB]

    def tiles(grad_ref, left_ref, right_ref, start, count):
        def one(t, carry):
            cut = pl.ds(pl.multiple_of(t * tile, tile), tile)
            grad_ref[:, cut] = dot(left_ref[...], right_ref[:, cut], 0, 0).astype(grad_ref.dtype)
            return carry

        lax.fori_loop(start, start + count, one, 0)

    @pl.when(jnp.logical_and(i >= swiglu, i < feed))
    def _():
        blocks = pair_of(i - swiglu, per)
        for s in blocks:
            norms.ready(s)
        gate, up, sig = opened(blocks)
        keep(a_ref, blocks, (gate * sig * up).astype(BF))

    at_step(feed - 1, copies[1].wait, lambda: tiles(gsh_ref, a_ref, dy_ref, 0, gsh_ref.shape[1] // tile))
    if line:
        at_step(feed, shrink.start)

    @pl.when(jnp.logical_and(i >= feed, i < feed + steps))
    def _():
        blocks = pair_of(i - feed, per)
        gate, up, sig = opened(blocks)
        dy, a = (jnp.concatenate([ref[rows_of(s), :] for s in blocks], axis=0) for ref in (dy_ref, a_ref))
        da = dot(dy, ws_ref[...], 1, 1)
        dgu = jnp.concatenate([da * up * (sig * (1.0 + gate * (1.0 - sig))), da * (gate * sig)], axis=1).astype(BF)
        keep(dgu_ref, blocks, dgu)
        put_pair(pulled_back, blocks, dot(dgu, we_ref[...], 1, 1).astype(BF))
        put_pair(branch, blocks, dot(a, ws_ref[...]).astype(BF))

    def grad_rows(s, at, summed):
        pulled, gain_grad = rms_pull(h_ref[at, :], gains_ref[:, d:2 * d], summed)
        dh = dy_ref[rows_of(s), :].astype(FP) + pulled
        dh_ref[at, :] = dh
        dg_ref[...] += fold_rows(gain_grad)
        stage[s % per] = dh.astype(BF)
        grads.send(s)

    def chip_rows(mine, k, summed):
        at = rows_of(k)

        @pl.when(mine)
        def _():
            base_ref[at, :] = h_ref[at, :] + summed

        @pl.when(jnp.logical_not(mine))
        def _():
            other_ref[k] = summed.astype(BF)

    in_turn(i, feed, steps, per, ((1, pulled_back.add_chip), (1, lambda s: branch.add(s, chip_rows)),
                                  (3, lambda s: pulled_back.take(s, grad_rows)), (5, grads.pass_on)))
    if line:
        for k in range(1, line):
            at_step(feed + k, lambda k=k: shrink.step(k))
    half = gex_ref.shape[1] // tile // 2
    at_step(feed + steps, lambda: tiles(gex_ref, xn_ref, dgu_ref, 0, half))
    at_step(feed + steps + 1, lambda: tiles(gex_ref, xn_ref, dgu_ref, half, half))

    @pl.when(i == feed + steps + 4)
    def _():
        attended.drain()
        pulled_back.drain()
        norms.drain()
        grads.drain()
        for t in range(4):
            branch.sent(t * per + per - 1)
        lax.fori_loop(0, 4 * per, lambda s, c: (grads.ready(s), c)[1], 0)
        if line:
            shrink.finish(write_to(gsh_out))
            shrink.drain()
            first.drain()
            second.drain()


def middle(q, k, vt, tags, bars, wm, x, dy, gains, weights, kv, group, unit, line):
    length = q.shape[0]
    n = LANES
    d = wm.shape[1]
    share = (length // 4, d)
    per = share[0] // SUB
    steps = 2 * per
    we, ws = (w.shape for w in weights)
    shards = 2 * line
    shrink = jax.ShapeDtypeStruct(ws, BF)
    more = []
    if line:
        shrink = jax.ShapeDtypeStruct(ws, FP)
        we, ws = (we[0] * shards, we[1]), (ws[0], ws[1] * shards)
        more = [pltpu.VMEM(ws, BF), *reduce_scratch(line, shrink.shape), *GATHER_SEMS(shards), *GATHER_SEMS(shards)]
    units = ws[0]
    results = [jax.ShapeDtypeStruct(q.shape, BF), jax.ShapeDtypeStruct((length // SUB, 8, SUB * group), FP),
               jax.ShapeDtypeStruct(share, FP), jax.ShapeDtypeStruct((per, SUB, d), BF), jax.ShapeDtypeStruct(we, BF),
               jax.ShapeDtypeStruct(share, FP), jax.ShapeDtypeStruct((length, d), BF), jax.ShapeDtypeStruct((8, d), FP),
               shrink]
    out_specs = [whole(r.shape) for r in results]
    out_specs[6] = ANYWHERE
    held = [q, k, vt, tags, bars, wm, gains]
    return pl.pallas_call(
        partial(middle_kernel, kv, group, unit, line, per, steps),
        grid=(3 * steps + 8,),
        in_specs=[whole(a.shape) for a in held] + [ANYWHERE] * 4,
        out_specs=out_specs,
        out_shape=results,
        scratch_shapes=[pltpu.VMEM((kv, n, SUB * group), FP), pltpu.VMEM((kv, 8, SUB * group), FP),
                        pltpu.VMEM(share, BF), pltpu.VMEM((length, d), BF), pltpu.VMEM(we, BF), pltpu.VMEM(ws, BF),
                        pltpu.SemaphoreType.DMA((4,)),
                        pltpu.VMEM(share, FP), pltpu.VMEM((length, d), BF), pltpu.VMEM((length, units), BF),
                        pltpu.VMEM((length, 2 * units), BF),
                        *pairs_scratch(per, d, True), pltpu.SemaphoreType.DMA((4, 4 * per)),
                        *pairs_scratch(per, d, True), pltpu.VMEM((per, SUB, d), BF),
                        pltpu.SemaphoreType.DMA((4, 4 * per)),
                        *pairs_scratch(per, d, False), *more],
        compiler_params=params(collective_id=1, has_side_effects=True),
        name="middle",
    )(*held, x, dy, *weights)


def back_kernel(kv, group, unit, scale, blocks, per, line, *refs):
    refs = list(refs)
    take = lambda count: [refs.pop(0) for _ in range(count)]
    q_ref, k_ref, v_ref, kt_ref, tags_ref, bars_ref, lse_ref, ctx_block, dh_block, wm_ref = take(10)
    raw_ref, cos_ref, sin_ref, all_gains, base_ref, dg2_ref, other_ref = take(7)
    x_all, dh_all = take(2)
    late_from = take(4)
    grads = take(1) if line else []
    in_ref, out_ref, gains_out = take(3)
    sums = take(3) if line else []
    weight_grads = [] if line else take(2)
    late_to = take(4)
    wp_ref, ctx_ref, dh_ref, xn_ref = late_to
    late_sem = take(1)[0]
    late = [pltpu.make_async_copy(a, b, late_sem.at[w]) for w, (a, b) in enumerate(zip(late_from, late_to))]
    dk_ref, dv_ref, dq_ref, dqkv_ref = take(4)
    b_far, b_sems, x_held, x_near, x_sems = take(5)
    mine_ref, far_ref, x_far, f_sems, x_ref, dh_own, own_sems, heads_ref, fold_ref = take(9)
    place = Place(line)
    i = pl.program_id(0)
    b = blocks - 1 - i
    n = LANES
    pairs = Pairs(place, per, x_held, x_near, x_sems, lambda s: s % x_held.shape[0])
    subs = ROWS // SUB
    share, d = x_ref.shape
    gq, gk = all_gains[:, 2 * d:2 * d + n], all_gains[:, 2 * d + n:]
    tile = 256
    tensors = lax.axis_size("tensor")
    mates = [(place.dp, (place.t + step) % tensors) for step in range(1, tensors)]
    peers = []
    own_rows = pl.ds(pl.multiple_of(place.t * share, share), share)
    own_copies = [pltpu.make_async_copy(x_all.at[own_rows, :], x_ref, own_sems.at[0]),
                  pltpu.make_async_copy(dh_all, dh_own, own_sems.at[1])]
    if line:
        shards = 2 * line
        gm_ref, gp_ref = take(2)
        expand = Reduce(place, grads[0], row_cut(grads[0].shape[0] // shards), *take(4))
        merge = Reduce(place, gm_ref, column_cut(gm_ref.shape[1] // shards), None, *take(3))
        project = Reduce(place, gp_ref, row_cut(gp_ref.shape[0] // shards), None, *take(3))
        shown, over, g_sems = take(3)
        peers = [((place.dp + step) % shards, place.t) for step in range(1, shards)]
    else:
        gp_ref, gm_ref = weight_grads

    def tiles(grad_ref, left_ref, right_ref):
        def one(t, carry):
            cut = pl.ds(pl.multiple_of(t * tile, tile), tile)
            grad_ref[:, cut] = dot(left_ref[...], right_ref[:, cut], 0, 0).astype(grad_ref.dtype)
            return carry

        lax.fori_loop(0, grad_ref.shape[1] // tile, one, 0)

    def project_rows(t):
        cut = pl.ds(pl.multiple_of(t * tile, tile), tile)
        gp_ref[cut, :] = dot(xn_ref[:, cut], dqkv_ref[...], 0, 0).astype(BF)

    def chip(k):
        return send(far_ref.at[k], x_far.at[k], f_sems.at[0, k], f_sems.at[1, k], place.chip)

    def branch(k):
        return send(other_ref.at[k], b_far.at[k], b_sems.at[0, k], b_sems.at[1, k], place.chip)

    @pl.when(i == 0)
    def _():
        barrier = pltpu.get_barrier_semaphore()
        for device in mates + peers:
            pl.semaphore_signal(barrier, inc=1, device_id=device, device_id_type=MESH)
        for copy in late:
            copy.start()
        pl.semaphore_wait(barrier, len(mates + peers))
        if line:
            expand.start()
        for k in range(per):
            branch(k).start()
        dk_ref[...] = jnp.zeros_like(dk_ref)
        dv_ref[...] = jnp.zeros_like(dv_ref)
        heads_ref[...] = jnp.zeros_like(heads_ref)

    @pl.when(i < blocks)
    def _():
        here = pl.ds(pl.multiple_of(b * ROWS, ROWS), ROWS)
        dctx = dot(dh_block[...], wm_ref[...], 1, 1).astype(BF)
        ctx, q = ctx_block[...], q_ref[...]
        bars = jnp.concatenate([bars_ref[...]] * group, axis=0)
        wide, queries, outward, centres, lses = [], [], [], [], []
        for h in range(kv):
            queries.append(stacked(q, h, group))
            wide.append(jnp.concatenate([queries[h], bars], axis=1))
            outward.append(stacked(dctx, h, group))
            both = outward[h].astype(FP) * stacked(ctx, h, group).astype(FP)
            centres.append(jnp.sum(both.T, axis=0, keepdims=True))
            lses.append(jnp.concatenate([lse_ref[u, h:h + 1, g * SUB:(g + 1) * SUB]
                                         for g in range(group) for u in range(ROWS // SUB)], axis=1))
        dq_ref[...] = jnp.zeros_like(dq_ref)

        def chunk(j, diagonal):
            at = pl.ds(pl.multiple_of(j * ROWS, ROWS), ROWS)
            tags = tags_ref[at, :]
            for h in range(kv):
                cut = slice(h * n, (h + 1) * n)
                keys = jnp.concatenate([k_ref[at, cut], tags], axis=1)
                p = jnp.exp2(dot(keys, wide[h], 1, 1) * unit - lses[h])
                if diagonal:
                    p = jnp.where(causal_tile(group), p, 0.0)
                dp = dot(v_ref[at, cut], outward[h], 1, 1)
                ds = (p * (dp - centres[h])).astype(BF)
                dv_ref[at, cut] += dot(p.astype(BF), outward[h])
                dk_ref[at, cut] += dot(ds, queries[h])
                dq_ref[h] += dot(kt_ref[cut, at], ds)

        lax.fori_loop(0, b, lambda j, c: (chunk(j, False), c)[1], 0)
        chunk(b, True)

        cosines, sines = cos_ref[...], sin_ref[...]
        pieces = []
        for h in range(kv):
            dq = dq_ref[h].T
            for c in range(group + 1):
                if c < group:
                    grad, gain, row = dq[c * ROWS:(c + 1) * ROWS] * scale, gq, 0
                else:
                    grad, gain, row = dk_ref[here, h * n:(h + 1) * n] * scale, gk, 1
                grad = grad * cosines - pltpu.roll(grad, n // 2, 1) * sines
                at = (h * (group + 1) + c) * n
                piece, gain_grad = rms_pull(raw_ref[:, at:at + n], gain, grad)
                heads_ref[row] += fold_rows(gain_grad)
                pieces.append(piece)
            pieces.append(dv_ref[here, h * n:(h + 1) * n])
        dqkv = jnp.concatenate(pieces, axis=1).astype(BF)
        dqkv_ref[here, :] = dqkv
        pl.when(i == 0)(late[0].wait)
        part = dot(dqkv, wp_ref[...], 1, 1).astype(BF)
        for u in range(subs):
            s = subs * b + u
            pairs.put(s, part[u * SUB:(u + 1) * SUB], (i >= 2, s + 2 * subs))

    def chip_rows(mine, k, summed):
        @pl.when(mine)
        def _():
            mine_ref[pl.ds(pl.multiple_of(k * SUB, SUB), SUB), :] = summed

        @pl.when(jnp.logical_not(mine))
        def _():
            far_ref[k] = summed.astype(BF)
            chip(k).start()

    @pl.when(i >= 1)
    def _():
        for u in range(subs):
            pairs.add(subs * (b + 1) + u, chip_rows)

    @pl.when(i == 3)
    def _():
        for k in range(per):
            branch(k).wait()
            at = slice(k * SUB, (k + 1) * SUB)
            out_ref[at, :] = (base_ref[at, :] + b_far[k].astype(FP)).astype(BF)
        for copy in own_copies:
            copy.start()

    @pl.when(i == 1)
    def _():
        late[1].wait()
        late[2].wait()
        tiles(gm_ref, ctx_ref, dh_ref)

    if line:
        for step, act in enumerate((lambda: expand.step(1), lambda: expand.step(2), lambda: expand.step(3), merge.start,
                                    lambda: merge.step(1), lambda: merge.step(2))):
            pl.when(i == step)(act)

    def input_rows(k):
        at = slice(k * SUB, (k + 1) * SUB)
        chip(k).wait()
        summed = mine_ref[at, :] + x_far[k].astype(FP)
        pulled, gain_grad = rms_pull(x_ref[at, :].astype(FP), all_gains[:, :d], summed)
        in_ref[at, :] = (dh_own[at, :] + pulled).astype(BF)
        fold_ref[...] += fold_rows(gain_grad)

    def folded(ref):
        pieces = [fold_ref[...], dg2_ref[...], heads_ref[0], heads_ref[1]]
        row = jnp.sum(jnp.concatenate(pieces, axis=1), axis=0, keepdims=True)
        count = row.shape[1] // n
        for j in range(count):
            ref[j:j + 1, :] = row[:, j * n:(j + 1) * n]
        ref[count:, :] = jnp.zeros((ref.shape[0] - count, n), FP)

    def show(buffer, me, devices, first):
        copies = [send(buffer.at[me], buffer.at[me], g_sems.at[0, first + step], g_sems.at[1, first + step], device)
                  for step, device in enumerate(devices, 1)]
        for copy in copies:
            copy.start()
        return copies

    def added(buffer, me, devices, first):
        count = len(devices) + 1
        for step in range(1, count):
            who = (me - step + count) % count
            send(buffer.at[who], buffer.at[who], g_sems.at[0, first + step], g_sems.at[1, first + step],
                 place.sibling).wait_recv()
        total = buffer[0]
        for who in range(1, count):
            total = total + buffer[who]
        return total

    @pl.when(i == blocks)
    def _():
        fold_ref[...] = jnp.zeros_like(fold_ref)
        late[3].wait()
        for copy in own_copies:
            copy.wait()
        if not line:
            tiles(gp_ref, xn_ref, dqkv_ref)
            for k in range(per):
                input_rows(k)
            folded(gains_out)
        else:
            project_rows(project.turn(0))
            project.start()
            for q in range(1, line):
                project_rows(project.turn(q))
            merge.step(3)
            expand.finish(write_to(sums[0]))
            project.step(1)
            merge.finish(write_to(sums[1]))
            project.step(2)
            for k in range(per):
                input_rows(k)
            folded(shown.at[place.t])
            copies = show(shown, place.t, mates, 0)
            project.step(3)
            over[place.dp] = added(shown, place.t, mates, 0)
            copies += show(over, place.dp, peers, tensors)
            project.finish(write_to(sums[2]))
            gains_out[...] = added(over, place.dp, peers, tensors)
            for copy in copies:
                copy.wait_send()
            for r in (expand, merge, project):
                r.drain()
        for s in range(2 * subs):
            pairs.sent(s)


def back(q, k, v, kt, tags, bars, lse, ctx, dh, wm, wp, raw, cosines, sines, gains, xn, base, dg2, other, x, dh_own,
         grads, kv, group, unit, scale, line):
    length = q.shape[0]
    n = LANES
    d = wm.shape[1]
    blocks = length // ROWS
    per = other.shape[0]
    share = base.shape
    block_of = lambda i: jnp.maximum(blocks - 1 - i, 0)
    rows = lambda w: pl.BlockSpec((ROWS, w), lambda i: (block_of(i), 0))
    late = [wp, ctx, dh, xn]
    gain_rows = (-(-(gains.shape[1] // n) // 8) * 8, n)
    scratch = [*[pltpu.VMEM(a.shape, BF) for a in late], pltpu.SemaphoreType.DMA((4,)),
               pltpu.VMEM((length, kv * n), FP), pltpu.VMEM((length, kv * n), FP),
               pltpu.VMEM((kv, n, ROWS * group), FP), pltpu.VMEM((length, wp.shape[1]), BF),
               pltpu.VMEM((per, SUB, d), BF), pltpu.SemaphoreType.DMA((2, per)),
               pltpu.VMEM((2 * ROWS // SUB, SUB, d), BF), pltpu.VMEM((2 * per, SUB, d), BF),
               pltpu.SemaphoreType.DMA((2, 4 * per)),
               pltpu.VMEM(share, FP), pltpu.VMEM((per, SUB, d), BF), pltpu.VMEM((per, SUB, d), BF),
               pltpu.SemaphoreType.DMA((2, per)), pltpu.VMEM(share, BF), pltpu.VMEM(share, FP),
               pltpu.SemaphoreType.DMA((2,)), pltpu.VMEM((2, 8, n), FP), pltpu.VMEM((8, d), FP)]
    results = [jax.ShapeDtypeStruct(share, BF), jax.ShapeDtypeStruct(share, BF), jax.ShapeDtypeStruct(gain_rows, FP)]
    if line:
        shards = 2 * line
        own = [(grads[0].shape[0] // shards, grads[0].shape[1]), (wm.shape[0], wm.shape[1] // shards),
               (wp.shape[0] // shards, wp.shape[1])]
        views = ((own[0][0], 2, own[0][1] // 2), own[1], (own[2][0], own[2][1] // n, n))
        results += [jax.ShapeDtypeStruct(s, FP) for s in views]
        scratch += [pltpu.VMEM(wm.shape, BF), pltpu.VMEM(wp.shape, BF)]
        for w, s in enumerate(own):
            scratch += reduce_scratch(line, s, w == 0)
        scratch += [pltpu.VMEM((4, *gain_rows), FP), pltpu.VMEM((shards, *gain_rows), FP),
                    pltpu.SemaphoreType.DMA((2, 4 + shards))]
    else:
        results += [jax.ShapeDtypeStruct(wp.shape, BF), jax.ShapeDtypeStruct(wm.shape, BF)]
    args = [q, k, v, kt, tags, bars, lse, ctx, dh, wm, raw, cosines, sines, gains, base, dg2]
    more = [other, x, dh_own, *late, *grads]
    specs = [whole(a.shape) for a in args] + [ANYWHERE] * len(more)
    for at in (0, 5, 7, 8, 10, 11, 12):
        specs[at] = rows(args[at].shape[1])
    specs[6] = pl.BlockSpec((ROWS // SUB, 8, SUB * group), lambda i: (block_of(i), 0, 0))
    return pl.pallas_call(
        partial(back_kernel, kv, group, unit, scale, blocks, per, line),
        grid=(blocks + 1,),
        in_specs=specs,
        out_specs=[whole(r.shape) for r in results],
        out_shape=results,
        scratch_shapes=scratch,
        compiler_params=params(collective_id=3, has_side_effects=True),
        name="back",
    )(*args, *more)


def adamw_step(weight, moment_one, moment_two, gradient, step_rate, decay):
    mean_next = BETA_ONE * moment_one + (1.0 - BETA_ONE) * gradient
    square_next = BETA_TWO * moment_two + (1.0 - BETA_TWO) * gradient * gradient
    mean_hat = mean_next / (1.0 - BETA_ONE**STEP)
    square_hat = square_next / (1.0 - BETA_TWO**STEP)
    weight_next = weight - step_rate * (mean_hat / (jnp.sqrt(square_hat) + EPS_ADAM) + decay * weight)
    return weight_next, mean_next, square_next


def shards(
    tokens, cotangent, parents, token_segment, tree_id,
    projection_weight, projection_first_moment, projection_second_moment,
    merge_master, merge_mean, merge_square,
    expand_master, expand_mean, expand_square,
    shrink_master, shrink_mean, shrink_square,
    gain_master, gain_mean, gain_square,
):
    x = tokens[0]
    dy = cotangent[0]
    length, d = x.shape
    d_own, kv, per, n = projection_weight.shape
    group = per - 2
    units = expand_master.shape[2]
    scale = n ** (-0.5)
    unit = scale * math.log2(math.e)
    line = 4 if lax.axis_size("dp") == 8 and d_own % LANES == 0 else 0
    if line:
        masters = (projection_weight.reshape(d_own, kv * per, n), merge_master, expand_master, shrink_master)
    else:
        wp, we = (lax.all_gather(w.astype(BF).reshape(d_own, -1), "dp", axis=0, tiled=True)
                  for w in (projection_weight, expand_master))
        wm, ws = (lax.all_gather(w.astype(BF), "dp", axis=1, tiled=True) for w in (merge_master, shrink_master))
        masters = (wp,)

    gains = gain_master[None]
    fronts = front(x, gains, token_segment, parents, tree_id, masters, kv, group, line)
    xn1, q, k, v, kt, vt, raw, tags, bars, cosines, sines = fronts[:11]
    if line:
        wp, wm, *low = fronts[11:]
    else:
        low = (we, ws)
    ctx, lse, base, other, expand_grad, dh, dhb, dg2, shrink_sum = middle(
        q, k, vt, tags, bars, wm, x, dy, gains, low, kv, group, unit, line)
    backs = back(q, k, v, kt, tags, bars, lse, ctx, dhb, wm, wp, raw, cosines, sines, gains, xn1,
                 base, dg2, other, x, dh, (expand_grad,) if line else (), kv, group, unit, scale, line)
    input_grad, output, gain_rows = backs[:3]
    if line:
        expand_sum, merge_sum, project_sum = backs[3:]
    else:
        gain_rows = lax.psum(gain_rows, ("dp", "tensor"))
        project_sum, expand_sum = (
            lax.psum_scatter(g, "dp", scatter_dimension=0, tiled=True) for g in (backs[3], expand_grad))
        merge_sum, shrink_sum = (
            lax.psum_scatter(g, "dp", scatter_dimension=1, tiled=True) for g in (backs[4], shrink_sum))
    output, input_grad = output[None], input_grad[None]
    gain_grad = gain_rows.reshape(-1)[:gain_master.shape[0]]

    outs = [output, input_grad]
    for weight, mean, square, grad, rate in (
        (projection_weight, projection_first_moment, projection_second_moment, project_sum, RATE_PROJECT),
        (merge_master, merge_mean, merge_square, merge_sum, RATE_MERGE),
        (expand_master, expand_mean, expand_square, expand_sum, RATE_EXPAND),
        (shrink_master, shrink_mean, shrink_square, shrink_sum, RATE_SHRINK),
    ):
        grad = grad.astype(FP).reshape(weight.shape)
        after, mean_next, square_next = adamw_step(weight, mean, square, grad, rate, DECAY)
        outs += [after, mean_next, square_next, after.astype(BF)]
    gain_next, gain_mean_next, gain_square_next = adamw_step(
        gain_master, gain_mean, gain_square, gain_grad, RATE_GAIN, 0.0)
    return (*outs, gain_mean_next, gain_square_next, gain_next)


def solution(mesh):
    tokens = P("dp", None, None)
    project = P("dp", "tensor", None, None)
    columns = P("tensor", "dp")
    expand = P("dp", None, "tensor")
    shared = P("dp", "tensor", None)
    return jax.shard_map(
        shards,
        mesh=mesh,
        in_specs=(tokens, tokens, P(), P("dp", None), P("dp"), *[project] * 3, *[columns] * 3, *[expand] * 3,
                  *[columns] * 3, P(), P(), P()),
        out_specs=(shared, shared, *[project] * 4, *[columns] * 4, *[expand] * 4, *[columns] * 4, P(), P(), P()),
        check_vma=False,
    )
```

profile of v0, /device:TPU:0, one launch (start us, length us, event | category | flops | bytes accessed | tf_op | source)
XLA Modules:
  0.0 277.0 jit_solution(12291465955308748809)
XLA Ops:
  1.3 1.3 broadcast_in_dim.9.refs_1_.refs_6_.refs_13_
  2.6 50.3 %front.1 = (bf16[1536,1024]{1,0:T(8,128)(2,1)}, bf16[1536,512]{1,0:T(8,128)(2,1)}, bf16[1536,256]{1,0:T(8,128)(2,1)}, bf16[1536,256]{1,0:T(8,128)(2,1)}, bf16[25...) custom-call(bf16[1536,1024]{1,0:T(8,128)(2,1)} %bitcast.11, ...), custom_call_target="tpu_custom_call" | custom-call | tf_op jit(solution)/shard_map/front/pallas_call | solution.py:586
  52.9 122.3 %middle.1 = (bf16[1536,512]{1,0:T(8,128)(2,1)}, f32[12,8,256]{2,1,0:T(8,128)}, f32[384,1024]{1,0:T(8,128)}, bf16[3,128,1024]{2,1,0:T(8,128)(2,1)}, bf16[1024,153...) custom-call(bf16[1536,512]{1,0:T(8,128)(2,1)} %get-tuple-element.51., ...), custom_call_target="tpu_custom_call" | custom-call | tf_op jit(solution)/shard_map/middle/pallas_call | solution.py:846
  175.2 0.0 copy-start.17
  175.2 0.0 copy-start.18
  175.3 0.0 copy-start.19
  175.3 0.0 copy-start.3
  175.3 0.0 copy-start.15
  175.3 0.0 copy-start.16
  175.3 0.0 copy-start.2
  175.3 0.0 copy-start.12
  175.3 0.0 copy-start.13
  175.3 88.9 %back.1 = (bf16[384,1024]{1,0:T(8,128)(2,1)}, bf16[384,1024]{1,0:T(8,128)(2,1)}, f32[24,128]{1,0:T(8,128)}, f32[128,2,768]{2,1,0:T(2,128)}, f32[512,128]{1,0:T(8,128)}, /*index=5*/f32[128,8,128]{2,1,0:T(8,128)}) custom-call(bf16[1536,512]{1,0:T(8,128)(2,1)} %get-tuple-element.51.refs_0_, bf16[1536,256]{1,0:T(8,128)(2,1)} %get-tuple-element.52.refs_1_, ...), custom_call_target="tpu_custom_call" | custom-call | tf_op jit(solution)/shard_map/back/pallas_call | solution.py:1150
  264.3 0.0 copy-start.1
  264.3 0.0 copy-start.9
  264.3 0.0 copy-start.10
  264.4 1.5 multiply_subtract_fusion.4
  265.8 2.0 fusion.10
  267.9 0.0 copy-start
  267.9 1.3 fusion.6
  269.2 2.0 fusion.12
  271.3 3.9 %fusion.8 = (bf16[128,2,768]{2,1,0:T(2,128)(2,1)}, f32[128,2,768]{2,1,0:T(2,128)}, f32[128,2,768]{2,1,0:T(2,128)}, f32[128,2,768]{2,1,0:T(2,128)}) fusion(f32[128,2,768]{2,1,0:T(2,128)S(1)} %copy-done, f32[128,2,768]{2,1,0:T(2,128)S(1)} %copy-done.8, f32[128,2,768]{2,1,0:T(2,128)S(1)} %copy-done.6, f32[128,2,768]{2,1,0:T(2,128)S(1)} %copy-done.7), kind=kLoop, calls=%fused_computation.21 | loop fusion | flops 2949120 | bytes 5898240 | tf_op jit(solution)/shard_map/convert_element_type | solution.py:1228
  275.2 0.9 copy.45
  276.1 0.9 copy.46
  (27 shorter events, 0.1 us)
Async XLA Ops:
  175.2 89.1 %copy-start.17 = (f32[2304]{0:T(1024)S(1)}, f32[2304]{0:T(1024)}, u32[]{:S(2)}) copy-start(f32[2304]{0:T(1024)} %param.38) | copy-start | bytes 27652
  175.2 89.1 %copy-start.18 = (f32[2304]{0:T(1024)S(1)}, f32[2304]{0:T(1024)}, u32[]{:S(2)}) copy-start(f32[2304]{0:T(1024)} %param.40) | copy-start | bytes 27652
  175.3 89.1 %copy-start.19 = (f32[2304]{0:T(1024)S(1)}, f32[2304]{0:T(1024)}, u32[]{:S(2)}) copy-start(f32[2304]{0:T(1024)} %param.39) | copy-start | bytes 27652
  175.3 90.6 %copy-start.3 = (f32[512,128]{1,0:T(8,128)S(1)}, f32[512,128]{1,0:T(8,128)}, u32[]{:S(2)}) copy-start(f32[512,128]{1,0:T(8,128)} %refs_7_.1) | copy-start | bytes 786436
  175.3 90.6 %copy-start.15 = (f32[512,128]{1,0:T(8,128)S(1)}, f32[512,128]{1,0:T(8,128)}, u32[]{:S(2)}) copy-start(f32[512,128]{1,0:T(8,128)} %param.30) | copy-start | bytes 786436
  175.3 90.5 %copy-start.16 = (f32[512,128]{1,0:T(8,128)S(1)}, f32[512,128]{1,0:T(8,128)}, u32[]{:S(2)}) copy-start(f32[512,128]{1,0:T(8,128)} %param.31) | copy-start | bytes 786436
  175.3 92.5 %copy-start.2 = (f32[768,128]{1,0:T(8,128)S(1)}, f32[768,128]{1,0:T(8,128)}, u32[]{:S(2)}) copy-start(f32[768,128]{1,0:T(8,128)} %refs_9_.1) | copy-start | bytes 1179652
  175.3 92.5 %copy-start.12 = (f32[768,128]{1,0:T(8,128)S(1)}, f32[768,128]{1,0:T(8,128)}, u32[]{:S(2)}) copy-start(f32[768,128]{1,0:T(8,128)} %param.36) | copy-start | bytes 1179652
  175.3 92.5 %copy-start.13 = (f32[768,128]{1,0:T(8,128)S(1)}, f32[768,128]{1,0:T(8,128)}, u32[]{:S(2)}) copy-start(f32[768,128]{1,0:T(8,128)} %param.37) | copy-start | bytes 1179652
  175.3 92.5 %copy-start.14 = (f32[768,128]{1,0:T(8,128)S(1)}, f32[768,128]{1,0:T(8,128)}, u32[]{:S(2)}) copy-start(f32[768,128]{1,0:T(8,128)} %get-tuple-element.79) | copy-start | bytes 1179652
  264.3 4.9 %copy-start.1 = (f32[128,2,4,128]{3,2,1,0:T(4,128)S(1)}, f32[128,2,4,128]{3,2,1,0:T(4,128)}, u32[]{:S(2)}) copy-start(f32[128,2,4,128]{3,2,1,0:T(4,128)} %param.26) | copy-start | bytes 1572868
  264.3 4.9 %copy-start.9 = (f32[128,2,4,128]{3,2,1,0:T(4,128)S(1)}, f32[128,2,4,128]{3,2,1,0:T(4,128)}, u32[]{:S(2)}) copy-start(f32[128,2,4,128]{3,2,1,0:T(4,128)} %param.27) | copy-start | bytes 1572868
  264.3 4.9 %copy-start.10 = (f32[128,2,4,128]{3,2,1,0:T(4,128)S(1)}, f32[128,2,4,128]{3,2,1,0:T(4,128)}, u32[]{:S(2)}) copy-start(f32[128,2,4,128]{3,2,1,0:T(4,128)} %param.28) | copy-start | bytes 1572868
  264.3 4.9 %copy-start.11 = (f32[128,8,128]{2,1,0:T(8,128)S(1)}, f32[128,8,128]{2,1,0:T(8,128)}, u32[]{:S(2)}) copy-start(f32[128,8,128]{2,1,0:T(8,128)} %get-tuple-element.76) | copy-start | bytes 1572868
  267.9 3.4 %copy-start = (f32[128,2,768]{2,1,0:T(2,128)S(1)}, f32[128,2,768]{2,1,0:T(2,128)}, u32[]{:S(2)}) copy-start(f32[128,2,768]{2,1,0:T(2,128)} %refs_8_.1) | copy-start | bytes 2359300
  267.9 3.4 %copy-start.6 = (f32[128,2,768]{2,1,0:T(2,128)S(1)}, f32[128,2,768]{2,1,0:T(2,128)}, u32[]{:S(2)}) copy-start(f32[128,2,768]{2,1,0:T(2,128)} %param.33) | copy-start | bytes 2359300
  267.9 3.4 %copy-start.7 = (f32[128,2,768]{2,1,0:T(2,128)S(1)}, f32[128,2,768]{2,1,0:T(2,128)}, u32[]{:S(2)}) copy-start(f32[128,2,768]{2,1,0:T(2,128)} %param.34) | copy-start | bytes 2359300
  267.9 3.4 %copy-start.8 = (f32[128,2,768]{2,1,0:T(2,128)S(1)}, f32[128,2,768]{2,1,0:T(2,128)}, u32[]{:S(2)}) copy-start(f32[128,2,768]{2,1,0:T(2,128)} %get-tuple-element.78) | copy-start | bytes 2359300
  271.2 4.0 %copy-start.5 = (bf16[384,1024]{1,0:T(8,128)(2,1)S(1)}, bf16[384,1024]{1,0:T(8,128)(2,1)}, u32[]{:S(2)}) copy-start(bf16[384,1024]{1,0:T(8,128)(2,1)} %get-tuple-element.74) | copy-start | bytes 2359300
  271.3 4.8 %copy-start.4 = (bf16[384,1024]{1,0:T(8,128)(2,1)S(1)}, bf16[384,1024]{1,0:T(8,128)(2,1)}, u32[]{:S(2)}) copy-start(bf16[384,1024]{1,0:T(8,128)(2,1)} %get-tuple-element.75) | copy-start | bytes 2359300
where the time goes:
time: 277 us
  Pallas kernels  262 us (95%)
  other arithmetic  10.7 us (4%)
  local copies, waits for them, and re-layouts  3.19 us (1%)
    pallas_call x1, Pallas kernels, middle(): pl.pallas_call(partial(middle_kernel, kv, group, unit, line, per, steps),...  122 us
    pallas_call x1, Pallas kernels, back(): pl.pallas_call(partial(back_kernel, kv, group, unit, scale, blocks, per,...  88.9 us
    pallas_call x1, Pallas kernels, front(): pl.pallas_call(partial(front_kernel, kv, group, line), grid=(length // RO...  50.3 us
    convert_element_type x4, other arithmetic, shards(): outs += [after, mean_next, square_next, after.astype(BF)]  9.22 us

commit v1 on v0

--- a/solution.py
+++ b/solution.py
@@ -624,9 +624,9 @@
     take = lambda count: [refs.pop(0) for _ in range(count)]
     q_ref, k_ref, vt_ref, tags_ref, bars_ref, wm_ref, gains_ref, x_all, dy_all = take(9)
     weights = take(2)
-    ctx_ref, lse_ref, base_ref, other_ref, gex_ref, dh_ref, dhb_ref, dg_ref, gsh_out = take(9)
+    ctx_out, lse_ref, base_ref, other_ref, gate_out, up_out, dh_ref, dhb_ref, dg_ref, gsh_out = take(10)
     acc_ref, sum_ref, x_ref, dy_ref, we_ref, ws_ref, copy_sems = take(7)
-    h_ref, xn_ref, a_ref, dgu_ref = take(4)
+    h_ref, xn_ref, a_ref, dgu_ref, ctx_ref, gup_ref = take(6)
     h_held, h_near, h_far, h_sems, xn_sems = take(5)
     d_held, d_near, d_far, d_sems, stage, dh_sems = take(6)
     b_held, b_near, b_sems = take(3)
@@ -647,12 +647,16 @@
     if line:
         gsh_ref = take(1)[0]
         shrink = Reduce(place, gsh_ref, column_cut(gsh_ref.shape[1] // (2 * line)), None, *take(3))
+        gate_ref = take(1)[0]
+        expand = Reduce(place, gate_ref, row_cut(gate_ref.shape[0] // (2 * line)), None, *take(3))
         cuts = (row_cut(weights[0].shape[0]), column_cut(weights[1].shape[1]))
         first, second = [Gather(place, weights[w], (we_ref, ws_ref)[w], cuts[w], *take(2)) for w in range(2)]
     else:
-        gsh_ref = gsh_out
+        gsh_ref, gate_ref = gsh_out, gate_out
         copies += [pltpu.make_async_copy(weights[0], we_ref, copy_sems.at[2]),
                    pltpu.make_async_copy(weights[1], ws_ref, copy_sems.at[3])]
+    written = [pltpu.make_async_copy(ctx_ref, ctx_out, copy_sems.at[4]),
+               pltpu.make_async_copy(gup_ref, up_out, copy_sems.at[5])]
     rows_of = lambda s: pl.ds(pl.multiple_of(s * SUB, SUB), SUB)
 
     def at_step(step, *acts):
@@ -720,6 +724,7 @@
         norms.send(s)
 
     at_step(1, copies[0].wait)
+    at_step(steps, written[0].start)
     in_turn(i, 0, steps, per, ((1, attended.add_chip), (3, lambda s: attended.take(s, hidden_rows)), (5, norms.pass_on)))
     swiglu, feed = steps + 3, 2 * steps + 3
     if line:
@@ -734,21 +739,18 @@
         at_step(swiglu, copies[2].wait, copies[3].wait)
 
 
-    def opened(blocks):
-        xn = jnp.concatenate([xn_ref[rows_of(s), :] for s in blocks], axis=0)
-        gu = dot(xn, we_ref[...])
-        gate, up = gu[:, :units], gu[:, units:]
-        sig = 1.0 / (1.0 + jnp.exp(-gate))
-        return gate, up, sig
+    def gathered(ref, blocks):
+        return jnp.concatenate([ref[rows_of(s), :] for s in blocks], axis=0)
 
     def keep(ref, blocks, values):
         for u, s in enumerate(blocks):
             ref[rows_of(s), :] = values[u * SUB:(u + 1) * SUB]
 
-    def tiles(grad_ref, left_ref, right_ref, start, count):
+    def tiles(grad_ref, left_ref, right_ref, start, count, after):
         def one(t, carry):
             cut = pl.ds(pl.multiple_of(t * tile, tile), tile)
-            grad_ref[:, cut] = dot(left_ref[...], right_ref[:, cut], 0, 0).astype(grad_ref.dtype)
+            there = pl.ds(pl.multiple_of((t + after) * tile, tile), tile)
+            grad_ref[:, cut] = dot(left_ref[...], right_ref[:, there], 0, 0).astype(grad_ref.dtype)
             return carry
 
         lax.fori_loop(start, start + count, one, 0)
@@ -758,23 +760,25 @@
         blocks = pair_of(i - swiglu, per)
         for s in blocks:
             norms.ready(s)
-        gate, up, sig = opened(blocks)
-        keep(a_ref, blocks, (gate * sig * up).astype(BF))
-
-    at_step(feed - 1, copies[1].wait, lambda: tiles(gsh_ref, a_ref, dy_ref, 0, gsh_ref.shape[1] // tile))
+        gu = dot(gathered(xn_ref, blocks), we_ref[...])
+        gate, up = gu[:, :units], gu[:, units:]
+        keep(a_ref, blocks, (gate / (1.0 + jnp.exp(-gate)) * up).astype(BF))
+        keep(dgu_ref, blocks, gu.astype(BF))
+
+    at_step(feed - 1, copies[1].wait, lambda: tiles(gsh_ref, a_ref, dy_ref, 0, gsh_ref.shape[1] // tile, 0))
     if line:
         at_step(feed, shrink.start)
 
     @pl.when(jnp.logical_and(i >= feed, i < feed + steps))
     def _():
         blocks = pair_of(i - feed, per)
-        gate, up, sig = opened(blocks)
-        dy, a = (jnp.concatenate([ref[rows_of(s), :] for s in blocks], axis=0) for ref in (dy_ref, a_ref))
-        da = dot(dy, ws_ref[...], 1, 1)
+        gu = gathered(dgu_ref, blocks).astype(FP)
+        gate, up = gu[:, :units], gu[:, units:]
+        sig = 1.0 / (1.0 + jnp.exp(-gate))
+        da = dot(gathered(dy_ref, blocks), ws_ref[...], 1, 1)
         dgu = jnp.concatenate([da * up * (sig * (1.0 + gate * (1.0 - sig))), da * (gate * sig)], axis=1).astype(BF)
         keep(dgu_ref, blocks, dgu)
         put_pair(pulled_back, blocks, dot(dgu, we_ref[...], 1, 1).astype(BF))
-        put_pair(branch, blocks, dot(a, ws_ref[...]).astype(BF))
 
     def grad_rows(s, at, summed):
         pulled, gain_grad = rms_pull(h_ref[at, :], gains_ref[:, d:2 * d], summed)
@@ -795,14 +799,25 @@
         def _():
             other_ref[k] = summed.astype(BF)
 
-    in_turn(i, feed, steps, per, ((1, pulled_back.add_chip), (1, lambda s: branch.add(s, chip_rows)),
-                                  (3, lambda s: pulled_back.take(s, grad_rows)), (5, grads.pass_on)))
+    in_turn(i, feed, steps, per, ((1, pulled_back.add_chip), (3, lambda s: pulled_back.take(s, grad_rows)),
+                                  (5, grads.pass_on)))
+
+    @pl.when(jnp.logical_and(i >= feed + 3, i < feed + 3 + steps))
+    def _():
+        blocks = pair_of(i - feed - 3, per)
+        put_pair(branch, blocks, dot(gathered(a_ref, blocks), ws_ref[...]).astype(BF))
+
+    in_turn(i, feed, steps, per, ((4, lambda s: branch.add(s, chip_rows)),))
     if line:
         for k in range(1, line):
             at_step(feed + k, lambda k=k: shrink.step(k))
-    half = gex_ref.shape[1] // tile // 2
-    at_step(feed + steps, lambda: tiles(gex_ref, xn_ref, dgu_ref, 0, half))
-    at_step(feed + steps + 1, lambda: tiles(gex_ref, xn_ref, dgu_ref, half, half))
+    half = units // tile
+    at_step(feed + steps, lambda: tiles(gate_ref, xn_ref, dgu_ref, 0, half, 0))
+    if line:
+        at_step(feed + steps, expand.start)
+        for k in range(1, line):
+            at_step(feed + steps + k, lambda k=k: expand.step(k))
+    at_step(feed + steps + 1, lambda: tiles(gup_ref, xn_ref, dgu_ref, 0, half, half), written[1].start)
 
     @pl.when(i == feed + steps + 4)
     def _():
@@ -813,9 +828,13 @@
         for t in range(4):
             branch.sent(t * per + per - 1)
         lax.fori_loop(0, 4 * per, lambda s, c: (grads.ready(s), c)[1], 0)
+        for copy in written:
+            copy.wait()
         if line:
             shrink.finish(write_to(gsh_out))
             shrink.drain()
+            expand.finish(write_to(gate_out))
+            expand.drain()
             first.drain()
             second.drain()
 
@@ -830,18 +849,23 @@
     we, ws = (w.shape for w in weights)
     shards = 2 * line
     shrink = jax.ShapeDtypeStruct(ws, BF)
+    gate = jax.ShapeDtypeStruct((we[0], we[1] // 2), BF)
     more = []
     if line:
         shrink = jax.ShapeDtypeStruct(ws, FP)
+        gate = jax.ShapeDtypeStruct(gate.shape, FP)
         we, ws = (we[0] * shards, we[1]), (ws[0], ws[1] * shards)
-        more = [pltpu.VMEM(ws, BF), *reduce_scratch(line, shrink.shape), *GATHER_SEMS(shards), *GATHER_SEMS(shards)]
+        more = [pltpu.VMEM(ws, BF), *reduce_scratch(line, shrink.shape), pltpu.VMEM((we[0], we[1] // 2), BF),
+                *reduce_scratch(line, gate.shape), *GATHER_SEMS(shards), *GATHER_SEMS(shards)]
     units = ws[0]
     results = [jax.ShapeDtypeStruct(q.shape, BF), jax.ShapeDtypeStruct((length // SUB, 8, SUB * group), FP),
-               jax.ShapeDtypeStruct(share, FP), jax.ShapeDtypeStruct((per, SUB, d), BF), jax.ShapeDtypeStruct(we, BF),
-               jax.ShapeDtypeStruct(share, FP), jax.ShapeDtypeStruct((length, d), BF), jax.ShapeDtypeStruct((8, d), FP),
+               jax.ShapeDtypeStruct(share, FP), jax.ShapeDtypeStruct((per, SUB, d), BF), gate,
+               jax.ShapeDtypeStruct((we[0], units), BF), jax.ShapeDtypeStruct(share, FP),
+               jax.ShapeDtypeStruct((length, d), BF), jax.ShapeDtypeStruct((8, d), FP),
                shrink]
     out_specs = [whole(r.shape) for r in results]
-    out_specs[6] = ANYWHERE
+    for at in (0, 5, 7):
+        out_specs[at] = ANYWHERE
     held = [q, k, vt, tags, bars, wm, gains]
     return pl.pallas_call(
         partial(middle_kernel, kv, group, unit, line, per, steps),
@@ -851,9 +875,9 @@
         out_shape=results,
         scratch_shapes=[pltpu.VMEM((kv, n, SUB * group), FP), pltpu.VMEM((kv, 8, SUB * group), FP),
                         pltpu.VMEM(share, BF), pltpu.VMEM((length, d), BF), pltpu.VMEM(we, BF), pltpu.VMEM(ws, BF),
-                        pltpu.SemaphoreType.DMA((4,)),
+                        pltpu.SemaphoreType.DMA((6,)),
                         pltpu.VMEM(share, FP), pltpu.VMEM((length, d), BF), pltpu.VMEM((length, units), BF),
-                        pltpu.VMEM((length, 2 * units), BF),
+                        pltpu.VMEM((length, 2 * units), BF), pltpu.VMEM(q.shape, BF), pltpu.VMEM((we[0], units), BF),
                         *pairs_scratch(per, d, True), pltpu.SemaphoreType.DMA((4, 4 * per)),
                         *pairs_scratch(per, d, True), pltpu.VMEM((per, SUB, d), BF),
                         pltpu.SemaphoreType.DMA((4, 4 * per)),
@@ -870,7 +894,7 @@
     raw_ref, cos_ref, sin_ref, all_gains, base_ref, dg2_ref, other_ref = take(7)
     x_all, dh_all = take(2)
     late_from = take(4)
-    grads = take(1) if line else []
+    grads = take(2) if line else []
     in_ref, out_ref, gains_out = take(3)
     sums = take(3) if line else []
     weight_grads = [] if line else take(2)
@@ -899,7 +923,7 @@
     if line:
         shards = 2 * line
         gm_ref, gp_ref = take(2)
-        expand = Reduce(place, grads[0], row_cut(grads[0].shape[0] // shards), *take(4))
+        expand = Reduce(place, grads[1], row_cut(grads[1].shape[0] // shards), *take(4))
         merge = Reduce(place, gm_ref, column_cut(gm_ref.shape[1] // shards), None, *take(3))
         project = Reduce(place, gp_ref, row_cut(gp_ref.shape[0] // shards), None, *take(3))
         shown, over, g_sems = take(3)
@@ -914,6 +938,10 @@
             return carry
 
         lax.fori_loop(0, grad_ref.shape[1] // tile, one, 0)
+
+    def write_up(values):
+        sums[0][:, 0, :] = grads[0][...]
+        sums[0][:, 1, :] = values
 
     def project_rows(t):
         cut = pl.ds(pl.multiple_of(t * tile, tile), tile)
@@ -1085,7 +1113,7 @@
             for q in range(1, line):
                 project_rows(project.turn(q))
             merge.step(3)
-            expand.finish(write_to(sums[0]))
+            expand.finish(write_up)
             project.step(1)
             merge.finish(write_to(sums[1]))
             project.step(2)
@@ -1130,9 +1158,9 @@
     results = [jax.ShapeDtypeStruct(share, BF), jax.ShapeDtypeStruct(share, BF), jax.ShapeDtypeStruct(gain_rows, FP)]
     if line:
         shards = 2 * line
-        own = [(grads[0].shape[0] // shards, grads[0].shape[1]), (wm.shape[0], wm.shape[1] // shards),
+        own = [grads[0].shape, (wm.shape[0], wm.shape[1] // shards),
                (wp.shape[0] // shards, wp.shape[1])]
-        views = ((own[0][0], 2, own[0][1] // 2), own[1], (own[2][0], own[2][1] // n, n))
+        views = ((own[0][0], 2, own[0][1]), own[1], (own[2][0], own[2][1] // n, n))
         results += [jax.ShapeDtypeStruct(s, FP) for s in views]
         scratch += [pltpu.VMEM(wm.shape, BF), pltpu.VMEM(wp.shape, BF)]
         for w, s in enumerate(own):
@@ -1144,6 +1172,8 @@
     args = [q, k, v, kt, tags, bars, lse, ctx, dh, wm, raw, cosines, sines, gains, base, dg2]
     more = [other, x, dh_own, *late, *grads]
     specs = [whole(a.shape) for a in args] + [ANYWHERE] * len(more)
+    if line:
+        specs[-2] = whole(grads[0].shape)
     for at in (0, 5, 7, 8, 10, 11, 12):
         specs[at] = rows(args[at].shape[1])
     specs[6] = pl.BlockSpec((ROWS // SUB, 8, SUB * group), lambda i: (block_of(i), 0, 0))
@@ -1200,17 +1230,17 @@
         wp, wm, *low = fronts[11:]
     else:
         low = (we, ws)
-    ctx, lse, base, other, expand_grad, dh, dhb, dg2, shrink_sum = middle(
+    ctx, lse, base, other, gate_sum, up_grad, dh, dhb, dg2, shrink_sum = middle(
         q, k, vt, tags, bars, wm, x, dy, gains, low, kv, group, unit, line)
     backs = back(q, k, v, kt, tags, bars, lse, ctx, dhb, wm, wp, raw, cosines, sines, gains, xn1,
-                 base, dg2, other, x, dh, (expand_grad,) if line else (), kv, group, unit, scale, line)
+                 base, dg2, other, x, dh, (gate_sum, up_grad) if line else (), kv, group, unit, scale, line)
     input_grad, output, gain_rows = backs[:3]
     if line:
         expand_sum, merge_sum, project_sum = backs[3:]
     else:
         gain_rows = lax.psum(gain_rows, ("dp", "tensor"))
         project_sum, expand_sum = (
-            lax.psum_scatter(g, "dp", scatter_dimension=0, tiled=True) for g in (backs[3], expand_grad))
+            lax.psum_scatter(g, "dp", scatter_dimension=0, tiled=True) for g in (backs[3], jnp.concatenate([gate_sum, up_grad], axis=1)))
         merge_sum, shrink_sum = (
             lax.psum_scatter(g, "dp", scatter_dimension=1, tiled=True) for g in (backs[4], shrink_sum))
     output, input_grad = output[None], input_grad[None]

time: 277 us -> 273 us (0.986)
  Pallas kernels: 262 us -> 256 us
    pallas_call x1, Pallas kernels: 88.9 us -> 81.1 us  [back(): pl.pallas_call(partial(back_kernel, kv, group, unit, scale, blocks, per,...]
where the time goes in v1:
time: 273 us
  Pallas kernels  256 us (94%)
  other arithmetic  10.8 us (4%)
  local copies, waits for them, and re-layouts  3.87 us (1%)
    pallas_call x1, Pallas kernels, middle(): pl.pallas_call(partial(middle_kernel, kv, group, unit, line, per, steps),...  125 us
    pallas_call x1, Pallas kernels, back(): pl.pallas_call(partial(back_kernel, kv, group, unit, scale, blocks, per,...  81.1 us
    pallas_call x1, Pallas kernels, front(): pl.pallas_call(partial(front_kernel, kv, group, line), grid=(length // RO...  50.3 us
    convert_element_type x4, other arithmetic, shards(): outs += [after, mean_next, square_next, after.astype(BF)]  9.34 us

profile of v1, /device:TPU:0, one launch (start us, length us, event | category | flops | bytes accessed | tf_op | source)
XLA Modules:
  0.0 272.6 jit_solution(17196084161558498118)
XLA Ops:
  1.3 1.3 broadcast_in_dim.9.refs_1_.refs_6_.refs_13_
  2.6 50.3 %front.1 = (bf16[1536,1024]{1,0:T(8,128)(2,1)}, bf16[1536,512]{1,0:T(8,128)(2,1)}, bf16[1536,256]{1,0:T(8,128)(2,1)}, bf16[1536,256]{1,0:T(8,128)(2,1)}, bf16[25...) custom-call(bf16[1536,1024]{1,0:T(8,128)(2,1)} %bitcast.11, ...), custom_call_target="tpu_custom_call" | custom-call | tf_op jit(solution)/shard_map/front/pallas_call | solution.py:586
  52.9 125.0 %middle.1 = (bf16[1536,512]{1,0:T(8,128)(2,1)}, f32[12,8,256]{2,1,0:T(8,128)}, f32[384,1024]{1,0:T(8,128)}, bf16[3,128,1024]{2,1,0:T(8,128)(2,1)}, f32[128,768]{...) custom-call(bf16[1536,512]{1,0:T(8,128)(2,1)} %get-tuple-element.52., ...), custom_call_target="tpu_custom_call" | custom-call | tf_op jit(solution)/shard_map/middle/pallas_call | solution.py:870
  178.0 0.0 copy-start.17
  178.0 0.0 copy-start.18
  178.0 0.0 copy-start.19
  178.0 0.0 copy-start.3
  178.0 0.0 copy-start.15
  178.0 0.0 copy-start.16
  178.0 81.1 %back.1 = (bf16[384,1024]{1,0:T(8,128)(2,1)}, bf16[384,1024]{1,0:T(8,128)(2,1)}, f32[24,128]{1,0:T(8,128)}, f32[128,2,768]{2,1,0:T(2,128)}, f32[512,128]{1,0:T(8,128)}, /*index=5*/f32[128,8,128]{2,1,0:T(8,128)}) custom-call(bf16[1536,512]{1,0:T(8,128)(2,1)} %get-tuple-element.52.refs_0_, bf16[1536,256]{1,0:T(8,128)(2,1)} %get-tuple-element.53.refs_1_, ...), custom_call_target="tpu_custom_call" | custom-call | tf_op jit(solution)/shard_map/back/pallas_call | solution.py:1180
  259.1 0.0 copy-start.2
  259.1 0.0 copy-start.12
  259.1 0.0 copy-start.13
  259.2 1.4 multiply_subtract_fusion.4
  260.7 0.0 copy-start.9
  260.7 0.0 copy-start.10
  260.7 2.1 fusion.10
  262.8 1.3 fusion.6
  264.2 2.0 fusion.12
  266.2 0.2 copy-done.8
  266.4 3.9 %fusion.8 = (bf16[128,2,768]{2,1,0:T(2,128)(2,1)}, f32[128,2,768]{2,1,0:T(2,128)}, f32[128,2,768]{2,1,0:T(2,128)}, f32[128,2,768]{2,1,0:T(2,128)}) fusion(f32[128,2,768]{2,1,0:T(2,128)S(1)} %copy-done, f32[128,2,768]{2,1,0:T(2,128)S(1)} %copy-done.8, f32[128,2,768]{2,1,0:T(2,128)S(1)} %copy-done.6, f32[128,2,768]{2,1,0:T(2,128)S(1)} %copy-done.7), kind=kLoop, calls=%fused_computation.21 | loop fusion | flops 2949120 | bytes 5898240 | tf_op jit(solution)/shard_map/convert_element_type | solution.py:1258
  270.3 0.9 copy.45
  271.2 0.5 copy-done.4
  271.7 0.9 copy.46
  (27 shorter events, 0.1 us)
Async XLA Ops:
  178.0 81.2 %copy-start.17 = (f32[2304]{0:T(1024)S(1)}, f32[2304]{0:T(1024)}, u32[]{:S(2)}) copy-start(f32[2304]{0:T(1024)} %param.38) | copy-start | bytes 27652
  178.0 81.2 %copy-start.18 = (f32[2304]{0:T(1024)S(1)}, f32[2304]{0:T(1024)}, u32[]{:S(2)}) copy-start(f32[2304]{0:T(1024)} %param.40) | copy-start | bytes 27652
  178.0 81.2 %copy-start.19 = (f32[2304]{0:T(1024)S(1)}, f32[2304]{0:T(1024)}, u32[]{:S(2)}) copy-start(f32[2304]{0:T(1024)} %param.39) | copy-start | bytes 27652
  178.0 82.6 %copy-start.3 = (f32[512,128]{1,0:T(8,128)S(1)}, f32[512,128]{1,0:T(8,128)}, u32[]{:S(2)}) copy-start(f32[512,128]{1,0:T(8,128)} %refs_7_.1) | copy-start | bytes 786436
  178.0 82.6 %copy-start.15 = (f32[512,128]{1,0:T(8,128)S(1)}, f32[512,128]{1,0:T(8,128)}, u32[]{:S(2)}) copy-start(f32[512,128]{1,0:T(8,128)} %param.30) | copy-start | bytes 786436
  178.0 82.6 %copy-start.16 = (f32[512,128]{1,0:T(8,128)S(1)}, f32[512,128]{1,0:T(8,128)}, u32[]{:S(2)}) copy-start(f32[512,128]{1,0:T(8,128)} %param.31) | copy-start | bytes 786436
  259.1 3.7 %copy-start.2 = (f32[768,128]{1,0:T(8,128)S(1)}, f32[768,128]{1,0:T(8,128)}, u32[]{:S(2)}) copy-start(f32[768,128]{1,0:T(8,128)} %refs_9_.1) | copy-start | bytes 1179652
  259.1 3.7 %copy-start.12 = (f32[768,128]{1,0:T(8,128)S(1)}, f32[768,128]{1,0:T(8,128)}, u32[]{:S(2)}) copy-start(f32[768,128]{1,0:T(8,128)} %param.36) | copy-start | bytes 1179652
  259.1 3.7 %copy-start.13 = (f32[768,128]{1,0:T(8,128)S(1)}, f32[768,128]{1,0:T(8,128)}, u32[]{:S(2)}) copy-start(f32[768,128]{1,0:T(8,128)} %param.37) | copy-start | bytes 1179652
  259.1 3.7 %copy-start.14 = (f32[768,128]{1,0:T(8,128)S(1)}, f32[768,128]{1,0:T(8,128)}, u32[]{:S(2)}) copy-start(f32[768,128]{1,0:T(8,128)} %get-tuple-element.81) | copy-start | bytes 1179652
  260.6 3.5 %copy-start.1 = (f32[128,2,4,128]{3,2,1,0:T(4,128)S(1)}, f32[128,2,4,128]{3,2,1,0:T(4,128)}, u32[]{:S(2)}) copy-start(f32[128,2,4,128]{3,2,1,0:T(4,128)} %param.26) | copy-start | bytes 1572868
  260.7 3.5 %copy-start.9 = (f32[128,2,4,128]{3,2,1,0:T(4,128)S(1)}, f32[128,2,4,128]{3,2,1,0:T(4,128)}, u32[]{:S(2)}) copy-start(f32[128,2,4,128]{3,2,1,0:T(4,128)} %param.27) | copy-start | bytes 1572868
  260.7 3.5 %copy-start.10 = (f32[128,2,4,128]{3,2,1,0:T(4,128)S(1)}, f32[128,2,4,128]{3,2,1,0:T(4,128)}, u32[]{:S(2)}) copy-start(f32[128,2,4,128]{3,2,1,0:T(4,128)} %param.28) | copy-start | bytes 1572868
  260.7 3.5 %copy-start.11 = (f32[128,8,128]{2,1,0:T(8,128)S(1)}, f32[128,8,128]{2,1,0:T(8,128)}, u32[]{:S(2)}) copy-start(f32[128,8,128]{2,1,0:T(8,128)} %get-tuple-element.78) | copy-start | bytes 1572868
  264.1 2.1 copy-start
  264.1 2.1 copy-start.6
  264.1 2.1 copy-start.7
  264.1 2.2 copy-start.8
  266.4 3.9 %copy-start.5 = (bf16[384,1024]{1,0:T(8,128)(2,1)S(1)}, bf16[384,1024]{1,0:T(8,128)(2,1)}, u32[]{:S(2)}) copy-start(bf16[384,1024]{1,0:T(8,128)(2,1)} %get-tuple-element.76) | copy-start | bytes 2359300
  270.3 1.4 copy-start.4

commit v2 on v1

--- a/solution.py
+++ b/solution.py
@@ -27,6 +27,7 @@
 ROWS = 256
 LANES = 128
 SUB = 128
+PARTS = 2
 MESH = pl.DeviceIdType.MESH
 BLOCKED = -1e30
 VMEM_LIMIT = 56 * 2**20
@@ -94,6 +95,33 @@
         src_ref=src, dst_ref=dst, send_sem=sent, recv_sem=arrived, device_id=device, device_id_type=MESH)
 
 
+class Several:
+    def __init__(self, copies):
+        self.copies = copies
+
+    def start(self):
+        for copy in self.copies:
+            copy.start()
+
+    def wait_send(self):
+        for copy in self.copies:
+            copy.wait_send()
+
+    def wait_recv(self):
+        for copy in self.copies:
+            copy.wait_recv()
+
+    def wait(self):
+        self.wait_send()
+        self.wait_recv()
+
+
+def send_split(src, dst, sems, device):
+    size = SUB // PARTS
+    rows = [pl.ds(part * size, size) for part in range(PARTS)]
+    return Several([send(src.at[rows[part], :], dst.at[rows[part], :], *sems(part), device) for part in range(PARTS)])
+
+
 def row_cut(size):
     return lambda j: (pl.ds(pl.multiple_of(j * size, size), size), slice(None))
 
@@ -314,8 +342,8 @@
         return pl.ds(pl.multiple_of(k * SUB, SUB), SUB)
 
     def to_chip(self, s):
-        return send(self.near.at[self.near_slot(s)], self.far.at[s % self.per], self.sems.at[2, s], self.sems.at[3, s],
-                    self.place.chip)
+        return send_split(self.near.at[self.near_slot(s)], self.far.at[s % self.per],
+                          lambda part: (self.sems.at[2 + 2 * part, s], self.sems.at[3 + 2 * part, s]), self.place.chip)
 
     def add_chip(self, s):
         def use(mine, k, summed):
@@ -356,7 +384,7 @@
 
 def pairs_scratch(per, d, exchange):
     rows = [pltpu.VMEM((4, SUB, d), BF), pltpu.VMEM((2 * per, SUB, d), BF)]
-    return rows + [pltpu.VMEM((per, SUB, d), BF)] * exchange + [pltpu.SemaphoreType.DMA((4 if exchange else 2, 4 * per))]
+    return rows + [pltpu.VMEM((per, SUB, d), BF)] * exchange + [pltpu.SemaphoreType.DMA((2 + 2 * PARTS * exchange, 4 * per))]
 
 
 class Spread:
@@ -370,11 +398,13 @@
         return self.rows(s) if self.stage is None else self.stage.at[s % self.per]
 
     def copy(self, kind, src, s):
-        device = (self.place.chip, self.place.sibling)[kind]
-        return send(src, self.rows(s), self.sems.at[kind, s], self.sems.at[2, s], device)
+        if kind == 0:
+            return send_split(src, self.rows(s), lambda part: (self.sems.at[3 + 2 * part, s], self.sems.at[4 + 2 * part, s]),
+                              self.place.chip)
+        return send(src, self.rows(s), self.sems.at[0, s], self.sems.at[1, s], self.place.sibling)
 
     def kept(self, s):
-        return pltpu.make_async_copy(self.source(s), self.rows(s), self.sems.at[3, s])
+        return pltpu.make_async_copy(self.source(s), self.rows(s), self.sems.at[2, s])
 
     def send(self, s):
         for kind in (0, 1):
@@ -392,7 +422,7 @@
     def pass_on(self, s):
         @pl.when(self.passes(s))
         def _():
-            self.copy(1, self.rows(s), s).wait_recv()
+            self.copy(0, self.rows(s), s).wait_recv()
             self.copy(1, self.rows(s), s).start()
 
     def ready(self, s):
@@ -878,9 +908,9 @@
                         pltpu.SemaphoreType.DMA((6,)),
                         pltpu.VMEM(share, FP), pltpu.VMEM((length, d), BF), pltpu.VMEM((length, units), BF),
                         pltpu.VMEM((length, 2 * units), BF), pltpu.VMEM(q.shape, BF), pltpu.VMEM((we[0], units), BF),
-                        *pairs_scratch(per, d, True), pltpu.SemaphoreType.DMA((4, 4 * per)),
+                        *pairs_scratch(per, d, True), pltpu.SemaphoreType.DMA((3 + 2 * PARTS, 4 * per)),
                         *pairs_scratch(per, d, True), pltpu.VMEM((per, SUB, d), BF),
-                        pltpu.SemaphoreType.DMA((4, 4 * per)),
+                        pltpu.SemaphoreType.DMA((3 + 2 * PARTS, 4 * per)),
                         *pairs_scratch(per, d, False), *more],
         compiler_params=params(collective_id=1, has_side_effects=True),
         name="middle",
@@ -948,10 +978,12 @@
         gp_ref[cut, :] = dot(xn_ref[:, cut], dqkv_ref[...], 0, 0).astype(BF)
 
     def chip(k):
-        return send(far_ref.at[k], x_far.at[k], f_sems.at[0, k], f_sems.at[1, k], place.chip)
+        return send_split(far_ref.at[k], x_far.at[k], lambda part: (f_sems.at[2 * part, k], f_sems.at[2 * part + 1, k]),
+                          place.chip)
 
     def branch(k):
-        return send(other_ref.at[k], b_far.at[k], b_sems.at[0, k], b_sems.at[1, k], place.chip)
+        return send_split(other_ref.at[k], b_far.at[k], lambda part: (b_sems.at[2 * part, k], b_sems.at[2 * part + 1, k]),
+                          place.chip)
 
     @pl.when(i == 0)
     def _():
@@ -1149,11 +1181,11 @@
     scratch = [*[pltpu.VMEM(a.shape, BF) for a in late], pltpu.SemaphoreType.DMA((4,)),
                pltpu.VMEM((length, kv * n), FP), pltpu.VMEM((length, kv * n), FP),
                pltpu.VMEM((kv, n, ROWS * group), FP), pltpu.VMEM((length, wp.shape[1]), BF),
-               pltpu.VMEM((per, SUB, d), BF), pltpu.SemaphoreType.DMA((2, per)),
+               pltpu.VMEM((per, SUB, d), BF), pltpu.SemaphoreType.DMA((2 * PARTS, per)),
                pltpu.VMEM((2 * ROWS // SUB, SUB, d), BF), pltpu.VMEM((2 * per, SUB, d), BF),
                pltpu.SemaphoreType.DMA((2, 4 * per)),
                pltpu.VMEM(share, FP), pltpu.VMEM((per, SUB, d), BF), pltpu.VMEM((per, SUB, d), BF),
-               pltpu.SemaphoreType.DMA((2, per)), pltpu.VMEM(share, BF), pltpu.VMEM(share, FP),
+               pltpu.SemaphoreType.DMA((2 * PARTS, per)), pltpu.VMEM(share, BF), pltpu.VMEM(share, FP),
                pltpu.SemaphoreType.DMA((2,)), pltpu.VMEM((2, 8, n), FP), pltpu.VMEM((8, d), FP)]
     results = [jax.ShapeDtypeStruct(share, BF), jax.ShapeDtypeStruct(share, BF), jax.ShapeDtypeStruct(gain_rows, FP)]
     if line:

time: 273 us -> 274 us (level)
  no operation moved by 1% of the time
where the time goes in v2:
time: 274 us; the launch traced here: 273 us
  Pallas kernels  257 us (94%)
  other arithmetic  10.8 us (4%)
  local copies, waits for them, and re-layouts  3.87 us (1%)
    pallas_call x1, Pallas kernels, middle(): pl.pallas_call(partial(middle_kernel, kv, group, unit, line, per, steps),...  126 us
    pallas_call x1, Pallas kernels, back(): pl.pallas_call(partial(back_kernel, kv, group, unit, scale, blocks, per,...  81 us
    pallas_call x1, Pallas kernels, front(): pl.pallas_call(partial(front_kernel, kv, group, line), grid=(length // RO...  50.3 us
    convert_element_type x4, other arithmetic, shards(): outs += [after, mean_next, square_next, after.astype(BF)]  9.34 us

profile of v2, /device:TPU:0, one launch (start us, length us, event | category | flops | bytes accessed | tf_op | source)
XLA Modules:
  0.0 273.5 jit_solution(17061378486211656045)
XLA Ops:
  1.3 1.3 broadcast_in_dim.9.refs_1_.refs_6_.refs_13_
  2.6 50.3 %front.1 = (bf16[1536,1024]{1,0:T(8,128)(2,1)}, bf16[1536,512]{1,0:T(8,128)(2,1)}, bf16[1536,256]{1,0:T(8,128)(2,1)}, bf16[1536,256]{1,0:T(8,128)(2,1)}, bf16[25...) custom-call(bf16[1536,1024]{1,0:T(8,128)(2,1)} %bitcast.11, ...), custom_call_target="tpu_custom_call" | custom-call | tf_op jit(solution)/shard_map/front/pallas_call | solution.py:616
  52.9 126.0 %middle.1 = (bf16[1536,512]{1,0:T(8,128)(2,1)}, f32[12,8,256]{2,1,0:T(8,128)}, f32[384,1024]{1,0:T(8,128)}, bf16[3,128,1024]{2,1,0:T(8,128)(2,1)}, f32[128,768]{...) custom-call(bf16[1536,512]{1,0:T(8,128)(2,1)} %get-tuple-element.52., ...), custom_call_target="tpu_custom_call" | custom-call | tf_op jit(solution)/shard_map/middle/pallas_call | solution.py:900
  179.0 0.0 copy-start.17
  179.0 0.0 copy-start.18
  179.0 0.0 copy-start.19
  179.0 0.0 copy-start.3
  179.0 0.0 copy-start.15
  179.0 0.0 copy-start.16
  179.1 81.0 %back.1 = (bf16[384,1024]{1,0:T(8,128)(2,1)}, bf16[384,1024]{1,0:T(8,128)(2,1)}, f32[24,128]{1,0:T(8,128)}, f32[128,2,768]{2,1,0:T(2,128)}, f32[512,128]{1,0:T(8,128)}, /*index=5*/f32[128,8,128]{2,1,0:T(8,128)}) custom-call(bf16[1536,512]{1,0:T(8,128)(2,1)} %get-tuple-element.52.refs_0_, bf16[1536,256]{1,0:T(8,128)(2,1)} %get-tuple-element.53.refs_1_, ...), custom_call_target="tpu_custom_call" | custom-call | tf_op jit(solution)/shard_map/back/pallas_call | solution.py:1212
  260.0 0.0 copy-start.2
  260.0 0.0 copy-start.12
  260.1 0.0 copy-start.13
  260.1 1.4 multiply_subtract_fusion.4
  261.6 0.0 copy-start.9
  261.6 0.0 copy-start.10
  261.6 2.1 fusion.10
  263.8 1.3 fusion.6
  265.1 2.0 fusion.12
  267.1 0.2 copy-done.8
  267.3 3.9 %fusion.8 = (bf16[128,2,768]{2,1,0:T(2,128)(2,1)}, f32[128,2,768]{2,1,0:T(2,128)}, f32[128,2,768]{2,1,0:T(2,128)}, f32[128,2,768]{2,1,0:T(2,128)}) fusion(f32[128,2,768]{2,1,0:T(2,128)S(1)} %copy-done, f32[128,2,768]{2,1,0:T(2,128)S(1)} %copy-done.8, f32[128,2,768]{2,1,0:T(2,128)S(1)} %copy-done.6, f32[128,2,768]{2,1,0:T(2,128)S(1)} %copy-done.7), kind=kLoop, calls=%fused_computation.21 | loop fusion | flops 2949120 | bytes 5898240 | tf_op jit(solution)/shard_map/convert_element_type | solution.py:1290
  271.2 0.9 copy.45
  272.1 0.5 copy-done.4
  272.6 0.9 copy.46
  (27 shorter events, 0.1 us)
Async XLA Ops:
  179.0 81.1 %copy-start.17 = (f32[2304]{0:T(1024)S(1)}, f32[2304]{0:T(1024)}, u32[]{:S(2)}) copy-start(f32[2304]{0:T(1024)} %param.38) | copy-start | bytes 27652
  179.0 81.1 %copy-start.18 = (f32[2304]{0:T(1024)S(1)}, f32[2304]{0:T(1024)}, u32[]{:S(2)}) copy-start(f32[2304]{0:T(1024)} %param.40) | copy-start | bytes 27652
  179.0 81.1 %copy-start.19 = (f32[2304]{0:T(1024)S(1)}, f32[2304]{0:T(1024)}, u32[]{:S(2)}) copy-start(f32[2304]{0:T(1024)} %param.39) | copy-start | bytes 27652
  179.0 82.5 %copy-start.3 = (f32[512,128]{1,0:T(8,128)S(1)}, f32[512,128]{1,0:T(8,128)}, u32[]{:S(2)}) copy-start(f32[512,128]{1,0:T(8,128)} %refs_7_.1) | copy-start | bytes 786436
  179.0 82.5 %copy-start.15 = (f32[512,128]{1,0:T(8,128)S(1)}, f32[512,128]{1,0:T(8,128)}, u32[]{:S(2)}) copy-start(f32[512,128]{1,0:T(8,128)} %param.30) | copy-start | bytes 786436
  179.0 82.5 %copy-start.16 = (f32[512,128]{1,0:T(8,128)S(1)}, f32[512,128]{1,0:T(8,128)}, u32[]{:S(2)}) copy-start(f32[512,128]{1,0:T(8,128)} %param.31) | copy-start | bytes 786436
  260.0 3.7 %copy-start.2 = (f32[768,128]{1,0:T(8,128)S(1)}, f32[768,128]{1,0:T(8,128)}, u32[]{:S(2)}) copy-start(f32[768,128]{1,0:T(8,128)} %refs_9_.1) | copy-start | bytes 1179652
  260.0 3.7 %copy-start.12 = (f32[768,128]{1,0:T(8,128)S(1)}, f32[768,128]{1,0:T(8,128)}, u32[]{:S(2)}) copy-start(f32[768,128]{1,0:T(8,128)} %param.36) | copy-start | bytes 1179652
  260.1 3.7 %copy-start.13 = (f32[768,128]{1,0:T(8,128)S(1)}, f32[768,128]{1,0:T(8,128)}, u32[]{:S(2)}) copy-start(f32[768,128]{1,0:T(8,128)} %param.37) | copy-start | bytes 1179652
  260.1 3.7 %copy-start.14 = (f32[768,128]{1,0:T(8,128)S(1)}, f32[768,128]{1,0:T(8,128)}, u32[]{:S(2)}) copy-start(f32[768,128]{1,0:T(8,128)} %get-tuple-element.81) | copy-start | bytes 1179652
  261.6 3.5 %copy-start.1 = (f32[128,2,4,128]{3,2,1,0:T(4,128)S(1)}, f32[128,2,4,128]{3,2,1,0:T(4,128)}, u32[]{:S(2)}) copy-start(f32[128,2,4,128]{3,2,1,0:T(4,128)} %param.26) | copy-start | bytes 1572868
  261.6 3.5 %copy-start.9 = (f32[128,2,4,128]{3,2,1,0:T(4,128)S(1)}, f32[128,2,4,128]{3,2,1,0:T(4,128)}, u32[]{:S(2)}) copy-start(f32[128,2,4,128]{3,2,1,0:T(4,128)} %param.27) | copy-start | bytes 1572868
  261.6 3.5 %copy-start.10 = (f32[128,2,4,128]{3,2,1,0:T(4,128)S(1)}, f32[128,2,4,128]{3,2,1,0:T(4,128)}, u32[]{:S(2)}) copy-start(f32[128,2,4,128]{3,2,1,0:T(4,128)} %param.28) | copy-start | bytes 1572868
  261.6 3.5 %copy-start.11 = (f32[128,8,128]{2,1,0:T(8,128)S(1)}, f32[128,8,128]{2,1,0:T(8,128)}, u32[]{:S(2)}) copy-start(f32[128,8,128]{2,1,0:T(8,128)} %get-tuple-element.78) | copy-start | bytes 1572868
  265.0 2.1 copy-start
  265.1 2.1 copy-start.6
  265.1 2.1 copy-start.7
  265.1 2.2 copy-start.8
  267.3 3.9 %copy-start.5 = (bf16[384,1024]{1,0:T(8,128)(2,1)S(1)}, bf16[384,1024]{1,0:T(8,128)(2,1)}, u32[]{:S(2)}) copy-start(bf16[384,1024]{1,0:T(8,128)(2,1)} %get-tuple-element.76) | copy-start | bytes 2359300
  271.2 1.4 copy-start.4
